TPU v7x, 128 devices: a whole 4x4x4 slice. The times are simulated.
128 devices in a mesh: row: 8 (over x, core), col: 16 (over y, z).
Axes of the slice: x: 4, y: 4, z: 4, core: 2. Of those that a mesh axis runs over, the one named last changes fastest.
Arguments:
- elevation: float32 [1024, 65536], P('row', 'col'), may hold values from -6 to 6
- row_spectra: float32 [2, 2, 1024], replicated, may hold values from -4 to 4, as said below
- col_spectra: float32 [2, 2, 65536], replicated, may hold values from -4 to 4, as said below
Outputs:
- correlations: float32 [2, 1024, 65536], P(None, 'row', 'col')
Inputs may be any that keep to these rules, and one draw needn't show every extreme that they name: `row_spectra`: each footprint's row spectrum is that of a real profile: entry 1024 - k is the complex conjugate of entry k. `col_spectra`: each footprint's column spectrum is that of a real profile: entry 65536 - k is the complex conjugate of entry k.
All inputs are finite; a program needn't handle non-finite values.
Results may differ from a plain program's by a relative error of at most 0.0001.
Values sent between devices are 32-bit elements; how exact they have to be, the bound alone decides.
A program may use at most 192 MiB of HBM per device.

v0:
```python
import math

import jax
import jax.numpy as jnp
from jax import lax
from jax.sharding import PartitionSpec as P

PRECISE = lax.Precision.HIGHEST
TWO_PI = 2.0 * math.pi


def dft_matrix(length, direction):
    positions = jnp.arange(length, dtype=jnp.int32)
    turn_count = positions[:, None] * positions[None, :] % length
    angles = TWO_PI / length * turn_count.astype(jnp.float32)
    return (jnp.cos(angles), direction * jnp.sin(angles))


def phase_table(turn_count, modulus, direction):
    angles = TWO_PI / modulus * (turn_count % modulus).astype(jnp.float32)
    return (jnp.cos(angles), direction * jnp.sin(angles))


def complex_mul(left_pair, right_pair):
    return (
        left_pair[0] * right_pair[0] - left_pair[1] * right_pair[1],
        left_pair[0] * right_pair[1] + left_pair[1] * right_pair[0],
    )


def complex_einsum(einsum_form, left_pair, right_pair):

    def product_of(first_op, second_op):
        return jnp.einsum(
            einsum_form, first_op, second_op, precision=PRECISE, preferred_element_type=jnp.float32
        )

    if len(left_pair) == 1:
        return (product_of(left_pair[0], right_pair[0]), product_of(left_pair[0], right_pair[1]))
    return (
        product_of(left_pair[0], right_pair[0]) - product_of(left_pair[1], right_pair[1]),
        product_of(left_pair[0], right_pair[1]) + product_of(left_pair[1], right_pair[0]),
    )


def long_dft(field_pair, direction):
    leading = field_pair[0].shape[:-1]
    length = field_pair[0].shape[-1]
    inner_len = 2 ** ((length.bit_length() - 1) // 2)
    outer_len = length // inner_len
    folded = tuple((member.reshape(leading + (inner_len, outer_len)) for member in field_pair))
    section_one = complex_einsum("...ba,bk->...ka", folded, dft_matrix(inner_len, direction))
    index_k = jnp.arange(inner_len, dtype=jnp.int32)[:, None]
    index_a = jnp.arange(outer_len, dtype=jnp.int32)[None, :]
    turned = complex_mul(section_one, phase_table(index_k * index_a, length, direction))
    second = complex_einsum("...ka,aj->...jk", turned, dft_matrix(outer_len, direction))
    return tuple((member.reshape(leading + (length,)) for member in second))


def row_dft(field_pair, direction):
    return complex_einsum("rc,rk->kc", field_pair, dft_matrix(field_pair[0].shape[0], direction))


def row_regroup(values, direction, inverse):
    rows_local, cols_local = values[0].shape
    axis_count = lax.axis_size("row")
    slot_width = cols_local // axis_count
    pieces = tuple((member.reshape(rows_local, axis_count, slot_width) for member in values))
    matrix = dft_matrix(axis_count, direction)

    def combine_rows(received):
        stacked = tuple(
            (member.reshape(axis_count, rows_local, member.shape[2]) for member in received)
        )
        mixed_up = complex_einsum("pri,pk->kri", stacked, matrix)
        flattened = tuple(
            (member.reshape(axis_count * rows_local, 1, member.shape[2]) for member in mixed_up)
        )
        if inverse:
            return lax.all_to_all(flattened, "row", split_axis=0, concat_axis=1, tiled=True)
        return lax.all_to_all(flattened, "row", split_axis=0, concat_axis=1, tiled=True)

    if inverse:
        result = combine_rows(
            (
                lax.all_to_all(pieces[0], "row", split_axis=1, concat_axis=0, tiled=True),
                lax.all_to_all(pieces[1], "row", split_axis=1, concat_axis=0, tiled=True),
            )
        )
    else:
        result = combine_rows(
            (lax.all_to_all(pieces[0], "row", split_axis=1, concat_axis=0, tiled=True),)
        )
    return tuple((member.reshape(rows_local, cols_local) for member in result))


def col_cross(values, direction, inverse):
    rows_local, cols_local = values[0].shape
    axis_count = lax.axis_size("col")
    slot_width = cols_local // axis_count
    pieces = tuple((member.reshape(rows_local, axis_count, slot_width) for member in values))
    matrix = dft_matrix(axis_count, direction)

    def combine_cols(received):
        mixed_up = complex_einsum("ipm,pk->ikm", received, matrix)
        if inverse:
            return (
                lax.all_to_all(mixed_up[0], "col", split_axis=1, concat_axis=1, tiled=True),
                lax.all_to_all(mixed_up[1], "col", split_axis=1, concat_axis=1, tiled=True),
            )
        return (
            lax.all_to_all(mixed_up[0], "col", split_axis=1, concat_axis=1, tiled=True),
            lax.all_to_all(mixed_up[1], "col", split_axis=1, concat_axis=1, tiled=True),
        )

    if inverse:
        result = combine_cols(
            (
                lax.all_to_all(pieces[0], "col", split_axis=1, concat_axis=1, tiled=True),
                lax.all_to_all(pieces[1], "col", split_axis=1, concat_axis=1, tiled=True),
            )
        )
    else:
        result = combine_cols(
            (
                lax.all_to_all(pieces[0], "col", split_axis=1, concat_axis=1, tiled=True),
                lax.all_to_all(pieces[1], "col", split_axis=1, concat_axis=1, tiled=True),
            )
        )
    return tuple((member.reshape(rows_local, cols_local) for member in result))


def footprint_gains(row_pick, col_pick):
    first_gain = complex_mul(
        (row_pick[0, 0][:, None], row_pick[0, 1][:, None]),
        (col_pick[0, 0][None, :], col_pick[0, 1][None, :]),
    )
    second_gain = complex_mul(
        (row_pick[1, 0][:, None], row_pick[1, 1][:, None]),
        (col_pick[1, 0][None, :], col_pick[1, 1][None, :]),
    )
    return (first_gain[0] - second_gain[1], first_gain[1] + second_gain[0])


def body(elevation, row_spectra, col_spectra):
    rows_local, cols_local = elevation.shape
    row_count = lax.axis_size("row")
    col_count = lax.axis_size("col")
    row_index = lax.axis_index("row")
    col_index = lax.axis_index("col")
    all_rows = rows_local * row_count
    all_cols = cols_local * col_count
    footprints = row_spectra.shape[0]
    local_row = jnp.arange(rows_local, dtype=jnp.int32)[:, None]
    local_col = jnp.arange(cols_local, dtype=jnp.int32)[None, :]
    spread = complex_mul(
        row_regroup((elevation,), -1.0, False), phase_table(local_row * row_index, all_rows, -1.0)
    )
    rows_done = row_dft(spread, -1.0)
    row_pick = lax.dynamic_index_in_dim(
        row_spectra.reshape(footprints, 2, rows_local, row_count), row_index, 3, False
    )
    crossed = col_cross(rows_done, -1.0, False)
    spectrum = long_dft(
        complex_mul(crossed, phase_table(local_col * col_index, all_cols, -1.0)), -1.0
    )
    col_pick = lax.dynamic_index_in_dim(
        col_spectra.reshape(footprints, 2, cols_local, col_count), col_index, 3, False
    )
    gain_grid = footprint_gains(row_pick, col_pick)
    filtered = long_dft(complex_mul(spectrum, gain_grid), 1.0)
    cols_done = col_cross(
        complex_mul(filtered, phase_table(local_col * col_index, all_cols, 1.0)), 1.0, True
    )
    rows_back = row_dft(cols_done, 1.0)
    finished = row_regroup(
        complex_mul(rows_back, phase_table(local_row * row_index, all_rows, 1.0)), 1.0, True
    )
    norm_factor = 1.0 / (all_rows * all_cols)
    return jnp.stack([finished[0] * norm_factor, finished[1] * norm_factor])


def solution(mesh):
    in_specs = (P("row", "col"), P(), P())
    out_specs = P(None, "row", "col")
    return jax.shard_map(body, mesh=mesh, in_specs=in_specs, out_specs=out_specs, check_vma=False)
```

profile of v0, /device:TPU:1, one launch (start us, length us, event | category | flops | bytes accessed | tf_op | source)
XLA Modules:
  0.0 621.7 jit_solution(12552306712390342089)
XLA Ops:
  3.7 32.3 %all_to_all.133 = f32[128,8,512]{2,0,1:T(8,128)S(1)} all-to-all(f32[128,8,512]{2,0,1:T(8,128)} %copy.142), channel_id=1, replica_groups=mesh['row'=8,'col'=16] {'row'}, dimensions={1} | all-to-all | bytes 4194304 | tf_op jit(solution)/shard_map/all_to_all | solution.py:92
  43.6 5.8 all-to-all-start.1
  57.0 18.8 %all-to-all-done.1 = f32[1024,1,512]{2,1,0:T(1,128)} async-done(((f32[1024,1,512]{2,1,0:T(1,128)}), f32[1024,1,512]{2,1,0:T(1,128)}, u32[]{:S(2)}, u32[]{:S(2)}) %all-to-all-start.1) | async-done | bytes 2097184 | tf_op jit(solution)/shard_map/all_to_all | solution.py:81
  75.8 5.3 all-to-all-start.2
  83.2 24.4 %all-to-all-done.2 = f32[1024,1,512]{2,1,0:T(1,128)} async-done(((f32[1024,1,512]{2,1,0:T(1,128)}), f32[1024,1,512]{2,1,0:T(1,128)}, u32[]{:S(2)}, u32[]{:S(2)}) %all-to-all-start.2) | async-done | bytes 2097184 | tf_op jit(solution)/shard_map/all_to_all | solution.py:81
  115.7 7.8 %all-to-all-start.4 = ((f32[128,16,256]{2,0,1:T(8,128)}), f32[128,16,256]{2,0,1:T(8,128)}, u32[]{:S(2)}, u32[]{:S(2)}) async-start(f32[128,16,256]{2,0,1:T(8,128)} %bitcast.243), calls=%async_computation.4 | async-start | bytes 4194304 | tf_op jit(solution)/shard_map/all_to_all | solution.py:127
  131.4 18.7 %all-to-all-done.4 = f32[128,16,256]{2,0,1:T(8,128)} async-done(((f32[128,16,256]{2,0,1:T(8,128)}), f32[128,16,256]{2,0,1:T(8,128)}, u32[]{:S(2)}, u32[]{:S(2)}) %all-to-all-start.4) | async-done | bytes 2097184 | tf_op jit(solution)/shard_map/all_to_all | solution.py:127
  150.0 5.5 all-to-all-start.3
  155.5 5.7 fusion.54
  161.3 19.4 %all-to-all-done.3 = f32[128,16,256]{2,0,1:T(8,128)S(1)} async-done(((f32[128,16,256]{2,0,1:T(8,128)}), f32[128,16,256]{2,0,1:T(8,128)S(1)}, u32[]{:S(2)}, u32[]{:S(2)}) %all-to-all-start.3) | async-done | bytes 2097184 | tf_op jit(solution)/shard_map/all_to_all | solution.py:126
  187.7 7.2 %all-to-all-start.5 = ((f32[128,16,256]{2,0,1:T(8,128)}), f32[128,16,256]{2,0,1:T(8,128)}, u32[]{:S(2)}, u32[]{:S(2)}) async-start(f32[128,16,256]{2,0,1:T(8,128)} %copy.154), calls=%async_computation.5 | async-start | bytes 4194304 | tf_op jit(solution)/shard_map/all_to_all | solution.py:112
  204.8 15.3 %all-to-all-done.5 = f32[128,16,256]{2,0,1:T(8,128)} async-done(((f32[128,16,256]{2,0,1:T(8,128)}), f32[128,16,256]{2,0,1:T(8,128)}, u32[]{:S(2)}, u32[]{:S(2)}) %all-to-all-start.5) | async-done | bytes 2097184 | tf_op jit(solution)/shard_map/all_to_all | solution.py:112
  220.1 7.5 %all-to-all-start.6 = ((f32[128,16,256]{2,0,1:T(8,128)}), f32[128,16,256]{2,0,1:T(8,128)S(1)}, u32[]{:S(2)}, u32[]{:S(2)}) async-start(f32[128,16,256]{2,0,1:T(8,128)} %copy.159), calls=%async_computation.6 | async-start | bytes 4194304 | tf_op jit(solution)/shard_map/all_to_all | solution.py:113
  232.8 7.8 %dynamic-slice_reduce_fusion = f32[2,2,4096]{2,1,0:T(2,128)S(1)} fusion(f32[2,2,4096,16]{3,2,1,0:T(8,128)} %reshape.453, s32[]{:T(128)S(6)} %select_n.192), kind=kLoop, calls=%fused_computation | loop fusion | bytes 131076 | tf_op jit(solution)/shard_map/jit(dynamic_index_in_dim)/dynamic_slice | solution.py:167
  245.2 7.6 %all-to-all-done.6 = f32[128,16,256]{2,0,1:T(8,128)S(1)} async-done(((f32[128,16,256]{2,0,1:T(8,128)}), f32[128,16,256]{2,0,1:T(8,128)S(1)}, u32[]{:S(2)}, u32[]{:S(2)}) %all-to-all-start.6) | async-done | bytes 2097184 | tf_op jit(solution)/shard_map/all_to_all | solution.py:113
  318.3 6.7 %all-to-all-start.8 = ((f32[128,16,256]{2,0,1:T(8,128)}), f32[128,16,256]{2,0,1:T(8,128)S(1)}, u32[]{:S(2)}, u32[]{:S(2)}) async-start(f32[128,16,256]{2,0,1:T(8,128)} %copy.182), calls=%async_computation.8 | async-start | bytes 4194304 | tf_op jit(solution)/shard_map/all_to_all | solution.py:120
  328.0 22.2 %all-to-all-done.8 = f32[128,16,256]{2,0,1:T(8,128)S(1)} async-done(((f32[128,16,256]{2,0,1:T(8,128)}), f32[128,16,256]{2,0,1:T(8,128)S(1)}, u32[]{:S(2)}, u32[]{:S(2)}) %all-to-all-start.8) | async-done | bytes 2097184 | tf_op jit(solution)/shard_map/all_to_all | solution.py:120
  351.5 7.1 %all-to-all-start.7 = ((f32[128,16,256]{2,0,1:T(8,128)}), f32[128,16,256]{2,0,1:T(8,128)S(1)}, u32[]{:S(2)}, u32[]{:S(2)}) async-start(f32[128,16,256]{2,0,1:T(8,128)} %copy.180), calls=%async_computation.7 | async-start | bytes 4194304 | tf_op jit(solution)/shard_map/all_to_all | solution.py:119
  358.7 5.7 fusion.22
  364.4 19.4 %all-to-all-done.7 = f32[128,16,256]{2,0,1:T(8,128)S(1)} async-done(((f32[128,16,256]{2,0,1:T(8,128)}), f32[128,16,256]{2,0,1:T(8,128)S(1)}, u32[]{:S(2)}, u32[]{:S(2)}) %all-to-all-start.7) | async-done | bytes 2097184 | tf_op jit(solution)/shard_map/all_to_all | solution.py:119
  390.8 7.6 %all-to-all-start.9 = ((f32[128,16,256]{2,0,1:T(8,128)}), f32[128,16,256]{2,0,1:T(8,128)}, u32[]{:S(2)}, u32[]{:S(2)}) async-start(f32[128,16,256]{2,0,1:T(8,128)} %copy.184), calls=%async_computation.9 | async-start | bytes 4194304 | tf_op jit(solution)/shard_map/all_to_all | solution.py:108
  408.3 15.4 %all-to-all-done.9 = f32[128,16,256]{2,0,1:T(8,128)} async-done(((f32[128,16,256]{2,0,1:T(8,128)}), f32[128,16,256]{2,0,1:T(8,128)}, u32[]{:S(2)}, u32[]{:S(2)}) %all-to-all-start.9) | async-done | bytes 2097184 | tf_op jit(solution)/shard_map/all_to_all | solution.py:108
  423.7 7.1 %all-to-all-start.10 = ((f32[128,16,256]{2,0,1:T(8,128)}), f32[128,16,256]{2,0,1:T(8,128)}, u32[]{:S(2)}, u32[]{:S(2)}) async-start(f32[128,16,256]{2,0,1:T(8,128)} %copy.188), calls=%async_computation.10 | async-start | bytes 4194304 | tf_op jit(solution)/shard_map/all_to_all | solution.py:109
  439.6 16.3 %all-to-all-done.10 = f32[128,16,256]{2,0,1:T(8,128)} async-done(((f32[128,16,256]{2,0,1:T(8,128)}), f32[128,16,256]{2,0,1:T(8,128)}, u32[]{:S(2)}, u32[]{:S(2)}) %all-to-all-start.10) | async-done | bytes 2097184 | tf_op jit(solution)/shard_map/all_to_all | solution.py:109
  467.6 9.4 %all-to-all-start.12 = ((f32[128,8,512]{2,0,1:T(8,128)}), f32[128,8,512]{2,0,1:T(8,128)S(1)}, u32[]{:S(2)}, u32[]{:S(2)}) async-start(f32[128,8,512]{2,0,1:T(8,128)} %bitcast.246), calls=%async_computation.12 | async-start | bytes 4194304 | tf_op jit(solution)/shard_map/all_to_all | solution.py:87
  480.1 23.2 %all-to-all-done.12 = f32[128,8,512]{2,0,1:T(8,128)S(1)} async-done(((f32[128,8,512]{2,0,1:T(8,128)}), f32[128,8,512]{2,0,1:T(8,128)S(1)}, u32[]{:S(2)}, u32[]{:S(2)}) %all-to-all-start.12) | async-done | bytes 2097184 | tf_op jit(solution)/shard_map/all_to_all | solution.py:87
  509.2 5.8 fusion.2
  515.0 20.6 %all-to-all-done.11 = f32[128,8,512]{2,0,1:T(8,128)S(1)} async-done(((f32[128,8,512]{2,0,1:T(8,128)}), f32[128,8,512]{2,0,1:T(8,128)S(1)}, u32[]{:S(2)}, u32[]{:S(2)}) %all-to-all-start.11) | async-done | bytes 2097184 | tf_op jit(solution)/shard_map/all_to_all | solution.py:86
  544.7 5.4 all-to-all-start.13
  562.3 14.2 %all-to-all-done.13 = f32[1024,1,512]{2,1,0:T(1,128)} async-done(((f32[1024,1,512]{2,1,0:T(1,128)}), f32[1024,1,512]{2,1,0:T(1,128)}, u32[]{:S(2)}, u32[]{:S(2)}) %all-to-all-start.13) | async-done | bytes 2097184 | tf_op jit(solution)/shard_map/all_to_all | solution.py:80
  586.9 20.3 %all-to-all-done.14 = f32[1024,1,512]{2,1,0:T(1,128)S(1)} async-done(((f32[1024,1,512]{2,1,0:T(1,128)}), f32[1024,1,512]{2,1,0:T(1,128)S(1)}, u32[]{:S(2)}, u32[]{:S(2)}) %all-to-all-start.14) | async-done | bytes 2097184 | tf_op jit(solution)/shard_map/all_to_all | solution.py:80
  615.7 5.6 copy.202
  (111 shorter events, 219.6 us)
Async XLA Ops:
  43.6 32.2 %all-to-all-start.1 = ((f32[1024,1,512]{2,1,0:T(1,128)}), f32[1024,1,512]{2,1,0:T(1,128)}, u32[]{:S(2)}, u32[]{:S(2)}) async-start(f32[1024,1,512]{2,1,0:T(1,128)} %copy.145), calls=%async_computation.1 | async-start | bytes 4194304 | tf_op jit(solution)/shard_map/all_to_all | solution.py:81
  75.8 31.7 %all-to-all-start.2 = ((f32[1024,1,512]{2,1,0:T(1,128)}), f32[1024,1,512]{2,1,0:T(1,128)}, u32[]{:S(2)}, u32[]{:S(2)}) async-start(f32[1024,1,512]{2,1,0:T(1,128)} %copy.148), calls=%async_computation.2 | async-start | bytes 4194304 | tf_op jit(solution)/shard_map/all_to_all | solution.py:81
  109.6 2.3 copy-start
  115.7 34.3 %all-to-all-start.4 = ((f32[128,16,256]{2,0,1:T(8,128)}), f32[128,16,256]{2,0,1:T(8,128)}, u32[]{:S(2)}, u32[]{:S(2)}) async-start(f32[128,16,256]{2,0,1:T(8,128)} %bitcast.243), calls=%async_computation.4 | async-start | bytes 4194304 | tf_op jit(solution)/shard_map/all_to_all | solution.py:127
  123.5 4.0 copy-start.1
  150.0 30.7 %all-to-all-start.3 = ((f32[128,16,256]{2,0,1:T(8,128)}), f32[128,16,256]{2,0,1:T(8,128)S(1)}, u32[]{:S(2)}, u32[]{:S(2)}) async-start(f32[128,16,256]{2,0,1:T(8,128)} %bitcast.244), calls=%async_computation.3 | async-start | bytes 4194304 | tf_op jit(solution)/shard_map/all_to_all | solution.py:126
  187.7 32.4 %all-to-all-start.5 = ((f32[128,16,256]{2,0,1:T(8,128)}), f32[128,16,256]{2,0,1:T(8,128)}, u32[]{:S(2)}, u32[]{:S(2)}) async-start(f32[128,16,256]{2,0,1:T(8,128)} %copy.154), calls=%async_computation.5 | async-start | bytes 4194304 | tf_op jit(solution)/shard_map/all_to_all | solution.py:112
  204.8 23.2 %copy-start.6 = (f32[2,2,65536]{2,1,0:T(2,128)S(1)}, f32[2,2,65536]{2,1,0:T(2,128)}, u32[]{:S(2)}) copy-start(f32[2,2,65536]{2,1,0:T(2,128)} %param.5) | copy-start | bytes 3145732
  220.1 32.8 %all-to-all-start.6 = ((f32[128,16,256]{2,0,1:T(8,128)}), f32[128,16,256]{2,0,1:T(8,128)S(1)}, u32[]{:S(2)}, u32[]{:S(2)}) async-start(f32[128,16,256]{2,0,1:T(8,128)} %copy.159), calls=%async_computation.6 | async-start | bytes 4194304 | tf_op jit(solution)/shard_map/all_to_all | solution.py:113
  232.8 8.6 %copy-start.7 = (f32[2,2,1024]{2,1,0:T(2,128)S(1)}, f32[2,2,1024]{2,1,0:T(2,128)}, u32[]{:S(2)}) copy-start(f32[2,2,1024]{2,1,0:T(2,128)} %param.4) | copy-start | bytes 49156
  318.3 31.9 %all-to-all-start.8 = ((f32[128,16,256]{2,0,1:T(8,128)}), f32[128,16,256]{2,0,1:T(8,128)S(1)}, u32[]{:S(2)}, u32[]{:S(2)}) async-start(f32[128,16,256]{2,0,1:T(8,128)} %copy.182), calls=%async_computation.8 | async-start | bytes 4194304 | tf_op jit(solution)/shard_map/all_to_all | solution.py:120
  350.2 1.3 copy-start.3
  351.5 32.2 %all-to-all-start.7 = ((f32[128,16,256]{2,0,1:T(8,128)}), f32[128,16,256]{2,0,1:T(8,128)S(1)}, u32[]{:S(2)}, u32[]{:S(2)}) async-start(f32[128,16,256]{2,0,1:T(8,128)} %copy.180), calls=%async_computation.7 | async-start | bytes 4194304 | tf_op jit(solution)/shard_map/all_to_all | solution.py:119
  390.8 32.9 %all-to-all-start.9 = ((f32[128,16,256]{2,0,1:T(8,128)}), f32[128,16,256]{2,0,1:T(8,128)}, u32[]{:S(2)}, u32[]{:S(2)}) async-start(f32[128,16,256]{2,0,1:T(8,128)} %copy.184), calls=%async_computation.9 | async-start | bytes 4194304 | tf_op jit(solution)/shard_map/all_to_all | solution.py:108
  423.7 32.3 %all-to-all-start.10 = ((f32[128,16,256]{2,0,1:T(8,128)}), f32[128,16,256]{2,0,1:T(8,128)}, u32[]{:S(2)}, u32[]{:S(2)}) async-start(f32[128,16,256]{2,0,1:T(8,128)} %copy.188), calls=%async_computation.10 | async-start | bytes 4194304 | tf_op jit(solution)/shard_map/all_to_all | solution.py:109
  457.9 4.0 copy-start.4
  467.6 35.7 %all-to-all-start.12 = ((f32[128,8,512]{2,0,1:T(8,128)}), f32[128,8,512]{2,0,1:T(8,128)S(1)}, u32[]{:S(2)}, u32[]{:S(2)}) async-start(f32[128,8,512]{2,0,1:T(8,128)} %bitcast.246), calls=%async_computation.12 | async-start | bytes 4194304 | tf_op jit(solution)/shard_map/all_to_all | solution.py:87
  503.3 1.3 copy-start.2
  504.6 30.9 %all-to-all-start.11 = ((f32[128,8,512]{2,0,1:T(8,128)}), f32[128,8,512]{2,0,1:T(8,128)S(1)}, u32[]{:S(2)}, u32[]{:S(2)}) async-start(f32[128,8,512]{2,0,1:T(8,128)} %bitcast.245), calls=%async_computation.11 | async-start | bytes 4194304 | tf_op jit(solution)/shard_map/all_to_all | solution.py:86
  544.7 31.8 %all-to-all-start.13 = ((f32[1024,1,512]{2,1,0:T(1,128)}), f32[1024,1,512]{2,1,0:T(1,128)}, u32[]{:S(2)}, u32[]{:S(2)}) async-start(f32[1024,1,512]{2,1,0:T(1,128)} %copy.195), calls=%async_computation.13 | async-start | bytes 4194304 | tf_op jit(solution)/shard_map/all_to_all | solution.py:80
  576.5 30.7 %all-to-all-start.14 = ((f32[1024,1,512]{2,1,0:T(1,128)}), f32[1024,1,512]{2,1,0:T(1,128)S(1)}, u32[]{:S(2)}, u32[]{:S(2)}) async-start(f32[1024,1,512]{2,1,0:T(1,128)} %copy.199), calls=%async_computation.14 | async-start | bytes 4194304 | tf_op jit(solution)/shard_map/all_to_all | solution.py:80
  608.8 3.1 copy-start.5
where the time goes:
time: 629 us; the launch traced here: 622 us
  waiting for transfers between devices  256 us (41%)
  matrix products  137 us (22%)
  starting transfers between devices  91.5 us (15%)
  local copies, waits for them, and re-layouts  88.6 us (14%)
  blocking collectives  32.3 us (5%)
  other arithmetic  15.1 us (2%)
    dot_general x38, matrix products, product_of(): jnp.einsum(einsum_form, first_op, second_op, precision=PRECISE, preferred...  137 us
    all_to_all x4, waiting for transfers between devices, combine_rows(): lax.all_to_all(flattened, 'row', split_axis=0, concat_axis=1, tiled=True)  77.7 us
    all_to_all x2, waiting for transfers between devices, col_cross(): lax.all_to_all(pieces[1], 'col', split_axis=1, concat_axis=1, tiled=True)  40.9 us
    all_to_all x2, waiting for transfers between devices, col_cross(): lax.all_to_all(pieces[0], 'col', split_axis=1, concat_axis=1, tiled=True)  38.8 us
    all_to_all x1, blocking collectives, row_regroup(): lax.all_to_all(pieces[0], 'row', split_axis=1, concat_axis=0, tiled=True)  32.3 us
    all_to_all x2, waiting for transfers between devices, combine_cols(): lax.all_to_all(mixed_up[0], 'col', split_axis=1, concat_axis=1, tiled=True)  30.7 us
    all_to_all x2, waiting for transfers between devices, combine_cols(): lax.all_to_all(mixed_up[1], 'col', split_axis=1, concat_axis=1, tiled=True)  24 us
    all_to_all x1, waiting for transfers between devices, row_regroup(): lax.all_to_all(pieces[1], 'row', split_axis=1, concat_axis=0, tiled=True)  23.2 us
  transfers between devices with their start and end apart: 14, of which 14 were waited for; matrix products, arithmetic and copies ran while one was open for 17% of the time, Pallas kernels for 0%

commit v1 on v0

v1 whole, which is shorter than its diff:
```python
import math

import jax
import jax.numpy as jnp
import ml_dtypes
import numpy as np
from jax import lax
from jax.experimental import pallas as pl
from jax.experimental.pallas import tpu as pltpu
from jax.sharding import PartitionSpec as P

MESH = pl.DeviceIdType.MESH
SIDE = 256
ROW_DEVICES = 8
COL_DEVICES = 16
ROWS = 1024
LOCAL_COLS = 4096
LANES = 128
BLOCKS = LOCAL_COLS // LANES
TILES = ROWS // ROW_DEVICES // 8
SLOTS = BLOCKS // ROW_DEVICES
YZ_STEPS = [(dy, dz) for dy in range(4) for dz in range(4) if (dy, dz) != (0, 0)]
X_STEPS = [(dx, dk) for dx in range(4) for dk in range(2) if (dx, dk) != (0, 0)]


def split_constant(values):
    high = values.astype(ml_dtypes.bfloat16)
    low = (values - high.astype(np.float64)).astype(ml_dtypes.bfloat16)
    return high, low


def dft_constants():
    index = np.arange(SIDE)
    angles = 2.0 * np.pi / SIDE * (np.outer(index, index) % SIDE)
    cos, sin = np.cos(angles), np.sin(angles)
    left = np.block([[cos, sin], [-sin, cos]])
    right = np.block([[cos, -sin], [sin, cos]])
    turn = 2.0 * np.pi / (SIDE * SIDE) * np.outer(index, index)
    return split_constant(left) + split_constant(right) + (
        np.cos(turn).astype(np.float32),
        np.sin(turn).astype(np.float32),
    )


def split(values):
    high = values.astype(jnp.bfloat16)
    low = (values - high.astype(jnp.float32)).astype(jnp.bfloat16)
    return high, low


def dot(left, right):
    return jnp.dot(left, right, preferred_element_type=jnp.float32)


def dot_split(left, right):
    return dot(left[0], right[0]) + (dot(left[1], right[0]) + dot(left[0], right[1]))


def kernel(
    elev, profiles, gains, fwd_hi, fwd_lo, inv_hi, inv_lo, turn_cos, turn_sin, out,
    mid, yz_in, yz_res, x_in, x_res, circ_hi, circ_lo, x_hi, x_lo,
    yz_send, yz_recv, x_send, x_recv, own_sem,
):
    row, col = lax.axis_index("row"), lax.axis_index("col")

    def yz_peer(step):
        y = lax.rem(col // 4 + step[0], 4)
        z = lax.rem(col % 4 + step[1], 4)
        return y * 4 + z

    def x_peer(step):
        return lax.rem(row // 2 + step[0], 4) * 2 + lax.rem(row % 2 + step[1], 2)

    barrier = pltpu.get_barrier_semaphore()
    for step in YZ_STEPS:
        pl.semaphore_signal(barrier, inc=1, device_id=(row, yz_peer(step)), device_id_type=MESH)
    for step in X_STEPS:
        pl.semaphore_signal(barrier, inc=1, device_id=(x_peer(step), col), device_id_type=MESH)
    pl.semaphore_wait(barrier, len(YZ_STEPS) + len(X_STEPS))

    def yz_copies(half, stage, source, target):
        return [
            pltpu.make_async_remote_copy(
                src_ref=source(yz_peer(step)), dst_ref=target,
                send_sem=yz_send.at[half, stage, i], recv_sem=yz_recv.at[half, stage, i],
                device_id=(row, yz_peer(step)), device_id_type=MESH,
            )
            for i, step in enumerate(YZ_STEPS)
        ]

    def x_copies(half, stage, source, target):
        return [
            pltpu.make_async_remote_copy(
                src_ref=source(x_peer(step)), dst_ref=target,
                send_sem=x_send.at[half, stage, i], recv_sem=x_recv.at[half, stage, i],
                device_id=(x_peer(step), col), device_id_type=MESH,
            )
            for i, step in enumerate(X_STEPS)
        ]

    def start(copies):
        for copy in copies:
            copy.start()

    def wait_recv(copies):
        for copy in copies:
            copy.wait_recv()

    def build_circulant(half):
        spread = jnp.broadcast_to(profiles[1 - half], (128, ROWS))
        high, low = split(pltpu.roll(spread, 0, 1, stride=1, stride_axis=0))
        circ_hi[...] = high
        circ_lo[...] = low

    def row_filter(half):
        for slot in range(SLOTS):
            lanes = slice(slot * LANES, (slot + 1) * LANES)
            high, low = split(x_in[half, :, :, slot].reshape(ROWS, LANES))
            for base in (0, ROWS):
                x_hi[base:base + ROWS, lanes] = high
                x_lo[base:base + ROWS, lanes] = low

        def block(i, carry):
            rows = pl.ds(pl.multiple_of(i * 128, 128), ROWS)
            result = dot_split((circ_hi[...], circ_lo[...]), (x_hi[rows, :], x_lo[rows, :]))
            for slot in range(SLOTS):
                x_res[half, i, :, slot] = result[:, slot * LANES:(slot + 1) * LANES].reshape(TILES, 8, LANES)
            return carry

        lax.fori_loop(0, ROW_DEVICES, block, 0)

    def col_filter(half):
        source = yz_in.at[half].reshape(SIDE * 16, LANES)
        result = yz_res.at[half].reshape(SIDE * 16, LANES)
        forward = (fwd_hi, fwd_lo)
        inverse = (inv_hi, inv_lo)

        def whole(pair):
            return pair[0][...], pair[1][...]

        def load_row(row_id):
            return jnp.concatenate(
                [source[pl.ds(8 * side + row_id, SIDE, stride=16), :] for side in range(2)], 1
            )

        def store_row(row_id, values):
            for side in range(2):
                result[pl.ds(8 * side + row_id, SIDE, stride=16), :] = values[:, side * LANES:(side + 1) * LANES]

        for pair in range(4):
            field = jnp.concatenate([load_row(2 * pair), load_row(2 * pair + 1)], 0)
            first = dot_split(whole(forward), split(field))
            real, imag = first[:SIDE], first[SIDE:]
            cos, sin = turn_cos[...], turn_sin[...]
            turned = jnp.concatenate([real * cos + imag * sin, imag * cos - real * sin], 1)
            second = dot_split(split(turned), whole(inverse))
            real, imag = second[:, :SIDE], second[:, SIDE:]
            gain_real, gain_imag = gains[half, 0], gains[half, 1]
            scaled = jnp.concatenate(
                [real * gain_real - imag * gain_imag, real * gain_imag + imag * gain_real], 1
            )
            third = dot_split(split(scaled), whole(forward))
            real, imag = third[:, :SIDE], third[:, SIDE:]
            turned = jnp.concatenate([real * cos - imag * sin, imag * cos + real * sin], 0)
            fourth = dot_split(whole(inverse), split(turned))
            store_row(2 * pair, fourth[:SIDE])
            store_row(2 * pair + 1, fourth[SIDE:])

    started = []
    for half in range(2):
        col_field = elev if half == 0 else mid.at[1]
        row_field = elev if half == 0 else mid.at[0]
        col_target = mid.at[0] if half == 0 else out.at[1]
        row_target = mid.at[1] if half == 0 else out.at[0]
        mine = pl.ds(SLOTS * row, SLOTS)

        ins_yz = yz_copies(half, 0, lambda peer: col_field.at[peer], yz_in.at[half, col])
        ins_x = x_copies(
            half, 0, lambda peer: row_field.at[:, pl.ds(SLOTS * peer, SLOTS)], x_in.at[half, row]
        )
        own_yz = pltpu.make_async_copy(col_field.at[col], yz_in.at[half, col], own_sem.at[half, 0])
        own_x = pltpu.make_async_copy(row_field.at[:, mine], x_in.at[half, row], own_sem.at[half, 1])
        start(ins_yz + ins_x + [own_yz, own_x])
        build_circulant(half)
        own_x.wait()
        wait_recv(ins_x)
        row_filter(half)
        outs_x = x_copies(half, 1, lambda peer: x_res.at[half, peer], row_target.at[:, mine])
        back_x = pltpu.make_async_copy(x_res.at[half, row], row_target.at[:, mine], own_sem.at[half, 2])
        start(outs_x + [back_x])
        own_yz.wait()
        wait_recv(ins_yz)
        col_filter(half)
        outs_yz = yz_copies(half, 1, lambda peer: yz_res.at[half, peer], col_target.at[col])
        back_yz = pltpu.make_async_copy(yz_res.at[half, col], col_target.at[col], own_sem.at[half, 3])
        start(outs_yz + [back_yz])
        back_x.wait()
        wait_recv(outs_x)
        back_yz.wait()
        wait_recv(outs_yz)
        started += ins_yz + ins_x + outs_x + outs_yz
    for copy in started:
        copy.wait_send()


def row_profiles(row_spectra):
    side = 32
    index = np.arange(side)
    inner = 2.0 * np.pi / side * (np.outer(index, index) % side)
    cos, sin = np.cos(inner).astype(np.float32), np.sin(inner).astype(np.float32)
    turn = 2.0 * np.pi / ROWS * np.outer(index, index)
    turn_cos, turn_sin = np.cos(turn).astype(np.float32), np.sin(turn).astype(np.float32)
    folded = row_spectra.reshape(2, 2, side, side)

    def product(form, left, right):
        return jnp.einsum(form, left, right, precision=lax.Precision.HIGHEST)

    real, imag = folded[:, 0], folded[:, 1]
    first_real = product("fba,bj->faj", real, cos) + product("fba,bj->faj", imag, sin)
    first_imag = product("fba,bj->faj", imag, cos) - product("fba,bj->faj", real, sin)
    real = first_real * turn_cos + first_imag * turn_sin
    imag = first_imag * turn_cos - first_real * turn_sin
    values = product("faj,ai->fij", real, cos) + product("faj,ai->fij", imag, sin)
    return values.reshape(2, 1, ROWS) * (1.0 / ROWS)


def body(elevation, row_spectra, col_spectra):
    tiles = elevation.reshape(TILES, 8, BLOCKS, LANES).transpose(0, 2, 1, 3)
    profiles = row_profiles(row_spectra)
    gains = col_spectra.reshape(2, 2, SIDE, SIDE).transpose(0, 1, 3, 2) * (1.0 / (SIDE * SIDE))
    field = (TILES, BLOCKS, 8, LANES)
    slots = (ROW_DEVICES, TILES, SLOTS, 8, LANES)
    vmem = pl.BlockSpec(memory_space=pltpu.VMEM)
    result = pl.pallas_call(
        kernel,
        out_shape=jax.ShapeDtypeStruct((2,) + field, jnp.float32),
        in_specs=[vmem] * 9,
        out_specs=vmem,
        scratch_shapes=[
            pltpu.VMEM((2,) + field, jnp.float32),
            pltpu.VMEM((2,) + field, jnp.float32),
            pltpu.VMEM((2,) + field, jnp.float32),
            pltpu.VMEM((2,) + slots, jnp.float32),
            pltpu.VMEM((2,) + slots, jnp.float32),
            pltpu.VMEM((128, ROWS), jnp.bfloat16),
            pltpu.VMEM((128, ROWS), jnp.bfloat16),
            pltpu.VMEM((2 * ROWS, SLOTS * SIDE), jnp.bfloat16),
            pltpu.VMEM((2 * ROWS, SLOTS * SIDE), jnp.bfloat16),
            pltpu.SemaphoreType.DMA((2, 2, len(YZ_STEPS))),
            pltpu.SemaphoreType.DMA((2, 2, len(YZ_STEPS))),
            pltpu.SemaphoreType.DMA((2, 2, len(X_STEPS))),
            pltpu.SemaphoreType.DMA((2, 2, len(X_STEPS))),
            pltpu.SemaphoreType.DMA((2, 4)),
        ],
        compiler_params=pltpu.CompilerParams(
            collective_id=0, has_side_effects=True, vmem_limit_bytes=58 * 2**20
        ),
    )(tiles, profiles, gains, *(jnp.asarray(table) for table in dft_constants()))
    return result.transpose(0, 1, 3, 2, 4).reshape((2,) + elevation.shape)


def solution(mesh):
    in_specs = (P("row", "col"), P(), P())
    out_specs = P(None, "row", "col")
    return jax.shard_map(body, mesh=mesh, in_specs=in_specs, out_specs=out_specs, check_vma=False)
```

time: 629 us -> 172 us (0.27)
  waiting for transfers between devices: 256 us -> 0 us
  Pallas kernels: 0 us -> 155 us
  matrix products: 137 us -> 5.35 us
  starting transfers between devices: 91.5 us -> 0 us
  local copies, waits for them, and re-layouts: 88.6 us -> 8.49 us
  blocking collectives: 32.3 us -> 0 us
  other arithmetic: 15.1 us -> 1.76 us
    all_to_all x14 -> x0, waiting for transfers between devices: 256 us -> none  [the longest x4 77.7 us: combine_rows(): lax.all_to_all(flattened, 'row', split_axis=0, concat_axis=1, tiled=True)]
    pallas_call x0 -> x1, Pallas kernels: none -> 155 us  [body(): pl.pallas_call(kernel, out_shape=jax.ShapeDtypeStruct((2,) + field, jnp.f...]
    dot_general x38 -> x6, matrix products: 137 us -> 5.35 us  [product(): return jnp.einsum(form, left, right, precision=lax.Precision.HIGHEST)]
    all_to_all x14 -> x0, starting transfers between devices: 91.5 us -> none  [the longest x4 21 us: combine_rows(): lax.all_to_all(flattened, 'row', split_axis=0, concat_axis=1, tiled=True)]
    all_to_all x1 -> x0, blocking collectives: 32.3 us -> none  [row_regroup(): lax.all_to_all(pieces[0], 'row', split_axis=1, concat_axis=0, tiled=True)]
    reshape x11 -> x1, local copies, waits for them, and re-layouts: 28.5 us -> 0.09 us  [row_profiles(): folded = row_spectra.reshape(2, 2, side, side)]
    sub x5 -> x0, local copies, waits for them, and re-layouts: 10.7 us -> none  [the longest x4 7.74 us: complex_einsum(): product_of(left_pair[0], right_pair[0])]
    add x5 -> x0, local copies, waits for them, and re-layouts: 9.34 us -> none  [the longest x4 7.54 us: complex_einsum(): product_of(left_pair[0], right_pair[1])]
  transfers between devices with their start and end apart: 14 -> 0, of which waited for: 14 -> 0; matrix products, arithmetic and copies ran while one was open for 17% -> 0% of each run, Pallas kernels for 0% -> 0%
where the time goes in v1:
time: 172 us; the launch traced here: 171 us
  Pallas kernels  155 us (90%)
  local copies, waits for them, and re-layouts  8.49 us (5%)
  matrix products  5.35 us (3%)
  other arithmetic  1.76 us (1%)
    pallas_call x1, Pallas kernels, body(): pl.pallas_call(kernel, out_shape=jax.ShapeDtypeStruct((2,) + field, jnp.f...  155 us
    unnamed x2, local copies, waits for them, and re-layouts  5.38 us
    dot_general x6, matrix products, product(): return jnp.einsum(form, left, right, precision=lax.Precision.HIGHEST)  5.35 us

profile of v1, /device:TPU:1, one launch (start us, length us, event | category | flops | bytes accessed | tf_op | source)
XLA Modules:
  0.0 170.7 jit_solution(12562273470091888021)
XLA Ops:
  0.0 0.7 copy.22
  0.7 0.1 reshape.30
  0.8 0.9 fusion.12
  1.7 0.9 fusion.2
  2.6 0.9 fusion.11
  3.5 0.9 fusion.3
  4.4 0.9 fusion.7
  5.3 0.9 fusion.1
  6.2 0.1 copy.25
  6.3 0.7 mul.57.profiles
  7.0 1.8 %broadcast_multiply_fusion = f32[2,2,65536]{2,1,0:T(2,128)S(1)} fusion(f32[2,2,65536]{2,1,0:T(2,128)} %param.19), kind=kLoop, calls=%fused_computation.7 | loop fusion | flops 262144 | bytes 2097152 | tf_op jit(solution)/shard_map/mul | solution.py:230
  8.8 0.9 mul.60
  9.7 1.3 copy.26
  11.0 155.0 %shard_map.163 = f32[2,16,32,8,128]{4,3,2,1,0:T(8,128)} custom-call(f32[16,32,8,128]{3,2,1,0:T(8,128)} %bitcast.35, f32[2,1,1024]{2,1,0:T(1,128)} %mul.57.profiles, f32[2,2,256,256]{3,2,1,0:T(8,128)} %bitcast.34, bf16[512,512]{1,0:T(8,128)(2,1)} %constant.28.clone.fwd_hi, bf16[512,512]{1,0:T(8,128)(2,1)} %constant.29.clone.fwd_lo, ...), custom_call_target="tpu_custom_call" | custom-call | tf_op jit(solution)/shard_map/pallas_call | solution.py:234
  166.0 4.7 %copy.32 = f32[2,128,4096]{2,1,0:T(8,128)} copy(f32[2,128,4096]{2,1,0:T(8,128)} %bitcast.33) | data formatting | bytes 8388608

commit v2 on v1

v2 whole, which is shorter than its diff:
```python
import ml_dtypes
import jax
import jax.numpy as jnp
import numpy as np
from jax import lax
from jax.experimental import pallas as pl
from jax.experimental.pallas import tpu as pltpu
from jax.sharding import PartitionSpec as P

MESH = pl.DeviceIdType.MESH
SIDE = 256
LANES = 128
ROW_DEVICES = 8
COL_DEVICES = 16
ROWS = 1024
LOCAL_COLS = 4096
BLOCKS = LOCAL_COLS // LANES
TILES = ROWS // ROW_DEVICES // 8
PARTS = 2
SLOTS = BLOCKS // ROW_DEVICES // PARTS
LINES = 8 // PARTS
HALVES = SIDE // LANES
STRIPS = LOCAL_COLS // SIDE
YZ_STEPS = [
    (1, 1), (3, 3), (2, 2), (1, 3), (3, 1), (2, 1), (1, 2), (2, 3),
    (3, 2), (2, 0), (0, 2), (1, 0), (0, 1), (3, 0), (0, 3),
]
X_STEPS = [(1, 0), (3, 0), (1, 1), (3, 1), (2, 0), (2, 1), (0, 1)]


def split_constant(values):
    high = values.astype(ml_dtypes.bfloat16)
    low = (values - high.astype(np.float64)).astype(ml_dtypes.bfloat16)
    return [high, low]


def dft_constants():
    index = np.arange(SIDE)
    angles = 2.0 * np.pi / SIDE * (np.outer(index, index) % SIDE)
    cos, sin = np.cos(angles), np.sin(angles)
    forward = np.block([[cos, sin], [-sin, cos]])
    inverse = np.block([[cos, -sin], [sin, cos]])
    matrices = np.stack(split_constant(forward) + split_constant(inverse))
    turn = 2.0 * np.pi / (SIDE * SIDE) * np.outer(index, index)
    turns = np.stack([np.cos(turn), np.sin(turn)]).astype(np.float32)
    low = np.arange(8)
    lane = np.arange(LANES)
    first = 2.0 * np.pi / ROWS * (
        low[None, :, None] * (LANES * low[:, None, None] + lane[None, None, :]) % ROWS
    )
    first = np.stack([np.cos(first), np.sin(first)]).astype(np.float32)
    second = 2.0 * np.pi / LANES * (np.outer(lane, lane) % LANES)
    second = (np.stack([np.cos(second), np.sin(second)]) / ROWS).astype(np.float32)
    return matrices, turns, first, second


def split(values):
    high = values.astype(jnp.bfloat16)
    low = (values - high.astype(jnp.float32)).astype(jnp.bfloat16)
    return high, low


def dot(left, right):
    return jnp.dot(left, right, preferred_element_type=jnp.float32)


def dot_precise(left, right):
    return jnp.dot(
        left, right, preferred_element_type=jnp.float32, precision=lax.Precision.HIGHEST
    )


def dot_split(left, right):
    return dot(left[0], right[0]) + (dot(left[1], right[0]) + dot(left[0], right[1]))


def interleave(first, second):
    merged = []
    count = max(len(first), len(second))
    for i in range(count):
        for member in (first, second):
            merged += member[len(member) * i // count:len(member) * (i + 1) // count]
    return merged


def kernel(
    elev_hbm, row_hbm, col_hbm, matrices_hbm, turns_hbm, first_hbm, second_hbm,
    out_row, out_col,
    elev, row_spec, col_spec, matrices, turns, first, second, gains, circ_hi, circ_lo,
    yz_pack, yz_in, yz_res, yz_mid, col_mid, x_in, x_res, row_mid, x_hi, x_lo,
    yz_send, yz_recv, x_send, x_recv, own_sem, load_sem,
):
    row, col = lax.axis_index("row"), lax.axis_index("col")

    def yz_peer(step):
        return lax.rem(col // 4 + step[0], 4) * 4 + lax.rem(col % 4 + step[1], 4)

    def x_peer(step):
        return lax.rem(row // 2 + step[0], 4) * 2 + lax.rem(row % 2 + step[1], 2)

    loads = [
        pltpu.make_async_copy(source, target, load_sem.at[i])
        for i, (source, target) in enumerate([
            (elev_hbm, elev), (row_hbm, row_spec), (first_hbm, first), (second_hbm, second),
            (col_hbm, col_spec), (matrices_hbm, matrices), (turns_hbm, turns),
        ])
    ]
    for load in loads:
        load.start()

    barrier = pltpu.get_barrier_semaphore()
    for step in YZ_STEPS:
        pl.semaphore_signal(barrier, inc=1, device_id=(row, yz_peer(step)), device_id_type=MESH)
    for step in X_STEPS:
        pl.semaphore_signal(barrier, inc=1, device_id=(x_peer(step), col), device_id_type=MESH)

    def yz_copies(half, stage, part, source, target):
        return [
            pltpu.make_async_remote_copy(
                src_ref=source(yz_peer(step)), dst_ref=target,
                send_sem=yz_send.at[half, stage, part, i], recv_sem=yz_recv.at[half, stage, part, i],
                device_id=(row, yz_peer(step)), device_id_type=MESH,
            )
            for i, step in enumerate(YZ_STEPS)
        ]

    def x_copies(half, stage, part, source, target):
        return [
            pltpu.make_async_remote_copy(
                src_ref=source(x_peer(step)), dst_ref=target,
                send_sem=x_send.at[half, stage, part, i], recv_sem=x_recv.at[half, stage, part, i],
                device_id=(x_peer(step), col), device_id_type=MESH,
            )
            for i, step in enumerate(X_STEPS)
        ]

    def start(copies):
        for copy in copies:
            copy.start()

    def wait_recv(copies):
        for copy in copies:
            copy.wait_recv()

    def lines(part):
        for line in range(LINES):
            for side in range(HALVES):
                yield line, side, pl.ds(8 * side + LINES * part + line, SIDE, stride=8 * HALVES)

    def pack(field, half, part):
        rows = field.reshape(SIDE * 8 * HALVES, LANES)
        for line, side, where in lines(part):
            yz_pack[half, part, :, line, side] = rows[where, :].reshape(COL_DEVICES, STRIPS, LANES)

    def unpack(part):
        rows = col_mid.reshape(SIDE * 8 * HALVES, LANES)
        for line, side, where in lines(part):
            rows[where, :] = yz_mid[part, :, line, side].reshape(SIDE, LANES)

    def build_circulant(foot):
        real = row_spec[foot, pl.ds(0, 8, stride=2), :]
        imag = row_spec[foot, pl.ds(1, 8, stride=2), :]
        turned_real = jnp.zeros((8, LANES), jnp.float32)
        turned_imag = jnp.zeros((8, LANES), jnp.float32)
        for i in range(8):
            cos, sin = first[0, i], first[1, i]
            turned_real += real[i:i + 1] * cos + imag[i:i + 1] * sin
            turned_imag += imag[i:i + 1] * cos - real[i:i + 1] * sin
        grid = dot_precise(turned_real, second[0]) + dot_precise(turned_imag, second[1])
        index = lax.broadcasted_iota(jnp.int32, (LANES, ROWS), 1)
        group = lax.broadcasted_iota(jnp.int32, (LANES, ROWS), 0)
        spread = dot_precise(grid, jnp.where(index // 8 == group, 1.0, 0.0))
        keep = index[:8] % 8 == group[:8]
        profile = jnp.sum(jnp.where(keep, spread, 0.0), axis=0, keepdims=True)
        rolled = pltpu.roll(jnp.broadcast_to(profile, (LANES, ROWS)), 0, 1, stride=1, stride_axis=0)
        circ_hi[foot], circ_lo[foot] = split(rolled)

    def build_gains(foot):
        for member in range(2):
            for side in range(HALVES):
                values = col_spec[foot, pl.ds(2 * side + member, SIDE, stride=4), :]
                gains[foot, member, side * LANES:(side + 1) * LANES, :] = values.T * (1.0 / (SIDE * SIDE))

    def row_filter(half, part, send):
        foot = 1 - half
        for slot in range(SLOTS):
            lanes = slice(slot * LANES, (slot + 1) * LANES)
            high, low = split(x_in[half, part, :, :, slot].reshape(ROWS, LANES))
            for base in (0, ROWS):
                x_hi[base:base + ROWS, lanes] = high
                x_lo[base:base + ROWS, lanes] = low
        for owner, copy in send:
            rows = pl.ds(pl.multiple_of(owner * LANES, LANES), ROWS)
            result = dot_split((circ_hi[foot], circ_lo[foot]), (x_hi[rows, :], x_lo[rows, :]))
            for slot in range(SLOTS):
                x_res[half, part, owner, :, slot] = result[:, slot * LANES:(slot + 1) * LANES].reshape(TILES, 8, LANES)
            copy.start()

    def col_filter(half, part):
        foot = half
        forward = (matrices[0], matrices[1])
        inverse = (matrices[2], matrices[3])
        cos, sin = turns[0], turns[1]
        gain_real, gain_imag = gains[foot, 0], gains[foot, 1]

        def load_line(line):
            return jnp.concatenate(
                [yz_in[half, part, :, line, side].reshape(SIDE, LANES) for side in range(HALVES)], 1
            )

        def store_line(line, values):
            for side in range(HALVES):
                yz_res[half, part, :, line, side] = values[:, side * LANES:(side + 1) * LANES].reshape(
                    COL_DEVICES, STRIPS, LANES
                )

        for line in range(0, LINES, 2):
            field = jnp.concatenate([load_line(line), load_line(line + 1)], 0)
            result = dot_split(forward, split(field))
            real, imag = result[:SIDE], result[SIDE:]
            field = jnp.concatenate([real * cos + imag * sin, imag * cos - real * sin], 1)
            result = dot_split(split(field), inverse)
            real, imag = result[:, :SIDE], result[:, SIDE:]
            field = jnp.concatenate(
                [real * gain_real - imag * gain_imag, real * gain_imag + imag * gain_real], 1
            )
            result = dot_split(split(field), forward)
            real, imag = result[:, :SIDE], result[:, SIDE:]
            field = jnp.concatenate([real * cos - imag * sin, imag * cos + real * sin], 0)
            result = dot_split(inverse, split(field))
            store_line(line, result[:SIDE])
            store_line(line + 1, result[SIDE:])

    started = []

    def row_part(part):
        return pl.ds(SLOTS * (PARTS * row + part), SLOTS)

    for half in range(2):
        first_half = half == 0
        row_field = elev if first_half else col_mid
        col_field = elev if first_half else row_mid
        row_target = row_mid if first_half else out_row
        col_target = yz_mid if first_half else out_col
        ins_yz, ins_x, own_yz, own_x = [], [], [], []
        for part in range(PARTS):
            ins_yz.append(yz_copies(
                half, 0, part, lambda peer: yz_pack.at[half, part, peer], yz_in.at[half, part, col]
            ))
            ins_x.append(x_copies(
                half, 0, part,
                lambda peer: row_field.at[:, pl.ds(SLOTS * (PARTS * peer + part), SLOTS)],
                x_in.at[half, part, row],
            ))
            own_yz.append(pltpu.make_async_copy(
                yz_pack.at[half, part, col], yz_in.at[half, part, col], own_sem.at[half, 0, part]
            ))
            own_x.append(pltpu.make_async_copy(
                row_field.at[:, row_part(part)], x_in.at[half, part, row], own_sem.at[half, 1, part]
            ))
        if first_half:
            loads[0].wait()
            for part in range(PARTS):
                pack(elev, half, part)
            pl.semaphore_wait(barrier, len(YZ_STEPS) + len(X_STEPS))
            for part in range(PARTS):
                start(interleave(ins_yz[part], ins_x[part]) + [own_yz[part], own_x[part]])
            for load in loads[1:]:
                load.wait()
            for foot in range(2):
                build_circulant(foot)
                build_gains(foot)
        else:
            back_yz[0].wait()
            wait_recv(outs_yz[0])
            unpack(0)
            for part in range(PARTS):
                back_x[part].wait()
                wait_recv(outs_x[part])
            for part in range(PARTS):
                pack(row_mid, half, part)
                start(ins_yz[part] + [own_yz[part]])
            back_yz[1].wait()
            wait_recv(outs_yz[1])
            unpack(1)
            for part in range(PARTS):
                start(ins_x[part] + [own_x[part]])

        outs_yz, outs_x, back_yz, back_x = [], [], [], []
        for part in range(PARTS):
            own_x[part].wait()
            wait_recv(ins_x[part])
            outs_x.append(x_copies(
                half, 1, part, lambda peer: x_res.at[half, part, peer], row_target.at[:, row_part(part)]
            ))
            back_x.append(pltpu.make_async_copy(
                x_res.at[half, part, row], row_target.at[:, row_part(part)], own_sem.at[half, 2, part]
            ))
            owners = [x_peer(step) for step in X_STEPS] + [row]
            row_filter(half, part, list(zip(owners, outs_x[part] + [back_x[part]])))

            own_yz[part].wait()
            wait_recv(ins_yz[part])
            col_filter(half, part)
            outs_yz.append(yz_copies(
                half, 1, part, lambda peer: yz_res.at[half, part, peer], col_target.at[part, col]
            ))
            back_yz.append(pltpu.make_async_copy(
                yz_res.at[half, part, col], col_target.at[part, col], own_sem.at[half, 3, part]
            ))
            start(outs_yz[part] + [back_yz[part]])
        for part in range(PARTS):
            started += ins_yz[part] + ins_x[part] + outs_yz[part] + outs_x[part]

    for part in range(PARTS):
        back_x[part].wait()
        wait_recv(outs_x[part])
        back_yz[part].wait()
        wait_recv(outs_yz[part])
    for copy in started:
        copy.wait_send()


def finish_kernel(row_ref, col_ref, out):
    tiles = row_ref.shape[0]
    out[0] = row_ref[...]
    rows = out.reshape(2 * tiles * BLOCKS * 8, LANES)
    for part in range(PARTS):
        for line in range(LINES):
            for side in range(HALVES):
                begin = tiles * BLOCKS * 8 + 8 * side + LINES * part + line
                rows[pl.ds(begin, tiles * STRIPS, stride=8 * HALVES), :] = col_ref[part, :, line, side].reshape(
                    tiles * STRIPS, LANES
                )


def body(elevation, row_spectra, col_spectra):
    tiles = elevation.reshape(TILES, 8, BLOCKS, LANES).transpose(0, 2, 1, 3)
    row_lines = row_spectra.reshape(2, 2, ROWS // LANES, LANES).transpose(0, 2, 1, 3)
    col_lines = col_spectra.reshape(2, 2, SIDE * HALVES, LANES).transpose(0, 2, 1, 3)
    inputs = [
        tiles,
        row_lines.reshape(2, 2 * ROWS // LANES, LANES),
        col_lines.reshape(2, 2 * SIDE * HALVES, LANES),
    ] + [jnp.asarray(table) for table in dft_constants()]
    field = (TILES, BLOCKS, 8, LANES)
    packed = (PARTS, COL_DEVICES, LINES, HALVES, STRIPS, LANES)
    slots = (PARTS, ROW_DEVICES, TILES, SLOTS, 8, LANES)
    anywhere = pl.BlockSpec(memory_space=pl.ANY)
    row_done, col_done = pl.pallas_call(
        kernel,
        out_shape=[jax.ShapeDtypeStruct(field, jnp.float32), jax.ShapeDtypeStruct(packed, jnp.float32)],
        in_specs=[anywhere] * len(inputs),
        out_specs=[anywhere] * 2,
        scratch_shapes=[pltpu.VMEM(member.shape, member.dtype) for member in inputs] + [
            pltpu.VMEM((2, 2, SIDE, SIDE), jnp.float32),
            pltpu.VMEM((2, LANES, ROWS), jnp.bfloat16),
            pltpu.VMEM((2, LANES, ROWS), jnp.bfloat16),
            pltpu.VMEM((2,) + packed, jnp.float32),
            pltpu.VMEM((2,) + packed, jnp.float32),
            pltpu.VMEM((2,) + packed, jnp.float32),
            pltpu.VMEM(packed, jnp.float32),
            pltpu.VMEM(field, jnp.float32),
            pltpu.VMEM((2,) + slots, jnp.float32),
            pltpu.VMEM((2,) + slots, jnp.float32),
            pltpu.VMEM(field, jnp.float32),
            pltpu.VMEM((2 * ROWS, SLOTS * LANES), jnp.bfloat16),
            pltpu.VMEM((2 * ROWS, SLOTS * LANES), jnp.bfloat16),
            pltpu.SemaphoreType.DMA((2, 2, PARTS, len(YZ_STEPS))),
            pltpu.SemaphoreType.DMA((2, 2, PARTS, len(YZ_STEPS))),
            pltpu.SemaphoreType.DMA((2, 2, PARTS, len(X_STEPS))),
            pltpu.SemaphoreType.DMA((2, 2, PARTS, len(X_STEPS))),
            pltpu.SemaphoreType.DMA((2, 4, PARTS)),
            pltpu.SemaphoreType.DMA((len(inputs),)),
        ],
        compiler_params=pltpu.CompilerParams(
            collective_id=0, has_side_effects=True, vmem_limit_bytes=58 * 2**20
        ),
    )(*inputs)
    steps = 4
    result = pl.pallas_call(
        finish_kernel,
        grid=(steps,),
        out_shape=jax.ShapeDtypeStruct((2,) + field, jnp.float32),
        in_specs=[
            pl.BlockSpec((TILES // steps,) + field[1:], lambda i: (i, 0, 0, 0)),
            pl.BlockSpec((PARTS, COL_DEVICES // steps) + packed[2:], lambda i: (0, i, 0, 0, 0, 0)),
        ],
        out_specs=pl.BlockSpec((2, TILES // steps) + field[1:], lambda i: (0, i, 0, 0, 0)),
    )(row_done, col_done)
    return result.transpose(0, 1, 3, 2, 4).reshape((2,) + elevation.shape)


def solution(mesh):
    in_specs = (P("row", "col"), P(), P())
    out_specs = P(None, "row", "col")
    return jax.shard_map(body, mesh=mesh, in_specs=in_specs, out_specs=out_specs, check_vma=False)
```

time: 172 us -> 117 us (0.68)
  Pallas kernels: 155 us -> 116 us
  local copies, waits for them, and re-layouts: 8.49 us -> 0 us
  matrix products: 5.35 us -> 0 us
  other arithmetic: 1.76 us -> 0 us
    pallas_call x1 -> x2, Pallas kernels: 155 us -> 116 us  [the longest x1 111 us: body(): pl.pallas_call(kernel, out_shape=[jax.ShapeDtypeStruct(field, jnp.float32...]
    unnamed x2 -> x0, local copies, waits for them, and re-layouts: 5.38 us -> none
    dot_general x6 -> x0, matrix products: 5.35 us -> none  [product(): return jnp.einsum(form, left, right, precision=lax.Precision.HIGHEST)]
    mul x4 -> x0, local copies, waits for them, and re-layouts: 3.01 us -> none  [the longest x2 2.25 us: body(): col_spectra.reshape(2, 2, SIDE, SIDE).transpose(0, 1, 3, 2)]
    mul x1 -> x0, other arithmetic: 1.76 us -> none  [body(): col_spectra.reshape(2, 2, SIDE, SIDE).transpose(0, 1, 3, 2)]
where the time goes in v2:
time: 117 us; the launch traced here: 116 us
  Pallas kernels  116 us (99%)
    pallas_call x1, Pallas kernels, body(): pl.pallas_call(kernel, out_shape=[jax.ShapeDtypeStruct(field, jnp.float32...  111 us
    pallas_call x1, Pallas kernels, body(): pl.pallas_call(finish_kernel, grid=(steps,), out_shape=jax.ShapeDtypeStru...  5.08 us

profile of v2, /device:TPU:1, one launch (start us, length us, event | category | flops | bytes accessed | tf_op | source)
XLA Modules:
  0.0 116.4 jit_solution(13179134353901917147)
XLA Ops:
  0.0 111.3 %shard_map.73 = (f32[16,32,8,128]{3,2,1,0:T(8,128)}, f32[2,16,4,2,16,128]{5,4,3,2,1,0:T(8,128)}) custom-call(f32[16,32,8,128]{3,2,1,0:T(8,128)} %bitcast.16, f32[2,16,128]{2,1,0:T(8,128)} %bitcast.18, f32[2,1024,128]{2,1,0:T(8,128)} %bitcast.17, bf16[4,512,512]{2,1,0:T(8,128)(2,1)} %constant.8.clone.matrices_hbm, f32[2,256,256]{2,1,0:T(8,128)} %constant.9.clone.turns_hbm, ...), custom_call_target="tpu_custom_call" | custom-call | tf_op jit(solution)/shard_map/pallas_call | solution.py:350
  111.3 5.1 %shard_map.74 = f32[2,16,32,8,128]{4,3,2,1,0:T(8,128)} custom-call(f32[16,32,8,128]{3,2,1,0:T(8,128)} %get-tuple-element.7.row_ref, f32[2,16,4,2,16,128]{5,4,3,2,1,0:T(8,128)} %get-tuple-element.8.col_ref), custom_call_target="tpu_custom_call" | custom-call | tf_op jit(solution)/shard_map/pallas_call | solution.py:381

commit v3 on v2

v3 whole, which is shorter than its diff:
```python
import ml_dtypes
import jax
import jax.numpy as jnp
import numpy as np
from jax import lax
from jax.experimental import pallas as pl
from jax.experimental.pallas import tpu as pltpu
from jax.sharding import PartitionSpec as P

MESH = pl.DeviceIdType.MESH
SIDE = 256
LANES = 128
ROW_DEVICES = 8
COL_DEVICES = 16
ROWS = 1024
LOCAL_COLS = 4096
BLOCKS = LOCAL_COLS // LANES
TILES = ROWS // ROW_DEVICES // 8
PARTS = 2
SLOTS = BLOCKS // ROW_DEVICES // PARTS
LINES = 8 // PARTS
HALVES = SIDE // LANES
STRIPS = LOCAL_COLS // SIDE
PAIRS = TILES // PARTS
YZ_STEPS = [
    (1, 1), (3, 3), (2, 2), (1, 3), (3, 1), (2, 1), (1, 2), (2, 3),
    (3, 2), (2, 0), (0, 2), (1, 0), (0, 1), (3, 0), (0, 3),
]
X_STEPS = [(1, 0), (3, 0), (1, 1), (3, 1), (2, 0), (2, 1), (0, 1)]


def split_constant(values):
    high = values.astype(ml_dtypes.bfloat16)
    low = (values - high.astype(np.float64)).astype(ml_dtypes.bfloat16)
    return [high, low]


def dft_constants():
    index = np.arange(SIDE)
    angles = 2.0 * np.pi / SIDE * (np.outer(index, index) % SIDE)
    cos, sin = np.cos(angles), np.sin(angles)
    forward = np.block([[cos, sin], [-sin, cos]])
    inverse = np.block([[cos, -sin], [sin, cos]])
    matrices = np.stack(split_constant(forward) + split_constant(inverse))
    turn = 2.0 * np.pi / (SIDE * SIDE) * np.outer(index, index)
    turns = np.stack([np.cos(turn), np.sin(turn)]).astype(np.float32)
    low = np.arange(8)
    lane = np.arange(LANES)
    first = 2.0 * np.pi / ROWS * (
        low[None, :, None] * (LANES * low[:, None, None] + lane[None, None, :]) % ROWS
    )
    first = np.stack([np.cos(first), np.sin(first)]).astype(np.float32)
    second = 2.0 * np.pi / LANES * (np.outer(lane, lane) % LANES)
    second = (np.stack([np.cos(second), np.sin(second)]) / ROWS).astype(np.float32)
    return matrices, turns, first, second


def split(values):
    high = values.astype(jnp.bfloat16)
    low = (values - high.astype(jnp.float32)).astype(jnp.bfloat16)
    return high, low


def dot(left, right):
    return jnp.dot(left, right, preferred_element_type=jnp.float32)


def dot_precise(left, right):
    return jnp.dot(
        left, right, preferred_element_type=jnp.float32, precision=lax.Precision.HIGHEST
    )


def dot_split(left, right):
    return dot(left[0], right[0]) + (dot(left[1], right[0]) + dot(left[0], right[1]))


def interleave(first, second):
    merged = []
    count = max(len(first), len(second))
    for i in range(count):
        for member in (first, second):
            merged += member[len(member) * i // count:len(member) * (i + 1) // count]
    return merged


def kernel(
    elev_hbm, row_hbm, col_hbm, matrices_hbm, turns_hbm, first_hbm, second_hbm,
    out,
    elev, row_spec, col_spec, matrices, turns, first, second, gains, circ_hi, circ_lo,
    yz_pack, yz_in, yz_res, yz_back, col_mid, x_in, x_res, row_mid, x_hi, x_lo,
    yz_send, yz_recv, x_send, x_recv, load_sem,
):
    row, col = lax.axis_index("row"), lax.axis_index("col")
    yz_peers = [
        lax.rem(col // 4 + step[0], 4) * 4 + lax.rem(col % 4 + step[1], 4) for step in YZ_STEPS
    ]
    x_peers = [
        lax.rem(row // 2 + step[0], 4) * 2 + lax.rem(row % 2 + step[1], 2) for step in X_STEPS
    ]

    barrier = pltpu.get_barrier_semaphore()
    for peer in x_peers:
        pl.semaphore_signal(barrier, inc=1, device_id=(peer, col), device_id_type=MESH)
    for peer in yz_peers:
        pl.semaphore_signal(barrier, inc=1, device_id=(row, peer), device_id_type=MESH)

    loads = [
        pltpu.make_async_copy(source, target, load_sem.at[i])
        for i, (source, target) in enumerate([
            (elev_hbm, elev), (row_hbm, row_spec), (first_hbm, first), (second_hbm, second),
            (col_hbm, col_spec), (matrices_hbm, matrices), (turns_hbm, turns),
        ])
    ]
    for load in loads:
        load.start()

    def yz_copies(half, stage, part, source, target, arrived):
        sent, received = yz_send.at[half, stage, part], yz_recv.at[half, stage, part]
        copies = [
            pltpu.make_async_remote_copy(
                src_ref=source(peer), dst_ref=target, send_sem=sent, recv_sem=received,
                device_id=(row, peer), device_id_type=MESH,
            )
            for peer in yz_peers
        ]
        shares = yz_pack.at[half, part].reshape(COL_DEVICES, LINES * HALVES, STRIPS, LANES)
        leaving = shares.at[pl.ds(0, COL_DEVICES - 1)]
        return (
            copies, pltpu.make_async_copy(source(col), target, received),
            pltpu.make_async_copy(arrived, arrived, received), pltpu.make_async_copy(leaving, leaving, sent),
        )

    def x_copies(half, stage, part, band, source, target, arrived, leaving):
        sent, received = x_send.at[half, stage, part, band], x_recv.at[half, stage, part, band]
        copies = [
            pltpu.make_async_remote_copy(
                src_ref=source(peer), dst_ref=target, send_sem=sent, recv_sem=received,
                device_id=(peer, col), device_id_type=MESH,
            )
            for peer in x_peers
        ]
        return (
            copies, pltpu.make_async_copy(source(row), target, received),
            pltpu.make_async_copy(arrived, arrived, received), pltpu.make_async_copy(leaving, leaving, sent),
        )

    def start(exchange):
        for copy in exchange[0] + [exchange[1]]:
            copy.start()

    def wait(exchange):
        exchange[2].wait()

    def wait_sent(exchanges):
        for exchange in exchanges:
            exchange[3].wait()

    def natural(part):
        for line in range(LINES):
            for side in range(HALVES):
                yield line, side, pl.ds(8 * side + LINES * part + line, SIDE, stride=8 * HALVES)

    def banded():
        for turn in range(PARTS):
            for line in range(LINES):
                for side in range(HALVES):
                    where = pl.ds(8 * side + LINES * turn + line, SIDE // PARTS, stride=8 * HALVES)
                    yield turn, line, side, where

    def pack_natural(part):
        rows = elev.reshape(SIDE * 8 * HALVES, LANES)
        for line, side, where in natural(part):
            yz_pack[0, part, :, :, line, side] = rows[where, :].reshape(PAIRS, PARTS, STRIPS, LANES)

    def pack_banded(part):
        rows = row_mid.at[part].reshape(PAIRS * BLOCKS * 8, LANES)
        for turn, line, side, where in banded():
            yz_pack[1, part, :, turn, line, side] = rows[where, :].reshape(PAIRS, STRIPS, LANES)

    def unpack_banded(part):
        rows = col_mid.at[part].reshape(PAIRS * BLOCKS * 8, LANES)
        for turn, line, side, where in banded():
            rows[where, :] = yz_back[0, part, :, turn, line, side].reshape(SIDE // PARTS, LANES)

    def unpack_natural(part):
        rows = out.at[1].reshape(SIDE * 8 * HALVES, LANES)
        for line, side, where in natural(part):
            rows[where, :] = yz_back[1, part, :, :, line, side].reshape(SIDE, LANES)

    def build_circulant(foot):
        real = row_spec[foot, pl.ds(0, 8, stride=2), :]
        imag = row_spec[foot, pl.ds(1, 8, stride=2), :]
        turned_real = jnp.zeros((8, LANES), jnp.float32)
        turned_imag = jnp.zeros((8, LANES), jnp.float32)
        for i in range(8):
            cos, sin = first[0, i], first[1, i]
            turned_real += real[i:i + 1] * cos + imag[i:i + 1] * sin
            turned_imag += imag[i:i + 1] * cos - real[i:i + 1] * sin
        grid = dot_precise(turned_real, second[0]) + dot_precise(turned_imag, second[1])
        index = lax.broadcasted_iota(jnp.int32, (LANES, ROWS), 1)
        group = lax.broadcasted_iota(jnp.int32, (LANES, ROWS), 0)
        spread = dot_precise(grid, jnp.where(index // 8 == group, 1.0, 0.0))
        keep = index[:8] % 8 == group[:8]
        profile = jnp.sum(jnp.where(keep, spread, 0.0), axis=0, keepdims=True)
        rolled = pltpu.roll(jnp.broadcast_to(profile, (LANES, ROWS)), 0, 1, stride=1, stride_axis=0)
        banded_row = lax.broadcasted_iota(jnp.int32, (LANES, LANES), 0)
        natural_row = lax.broadcasted_iota(jnp.int32, (LANES, LANES), 1)
        source = banded_row % 64 // LINES * 8 + banded_row // 64 * LINES + banded_row % LINES
        for target, values in zip((circ_hi, circ_lo), split(rolled)):
            if foot == 1:
                order = jnp.where(source == natural_row, 1.0, 0.0).astype(jnp.bfloat16)
                target[foot] = dot(order, values).astype(jnp.bfloat16)
            else:
                source_column = natural_row % 64 // LINES * 8 + natural_row // 64 * LINES + natural_row % LINES
                order = jnp.where(source_column == banded_row, 1.0, 0.0).astype(jnp.bfloat16)
                for block in range(ROW_DEVICES):
                    lanes = slice(block * LANES, (block + 1) * LANES)
                    target[foot, :, lanes] = dot(values[:, lanes], order).astype(jnp.bfloat16)

    def build_gains(foot):
        for member in range(2):
            for side in range(HALVES):
                values = col_spec[foot, pl.ds(2 * side + member, SIDE, stride=4), :]
                gains[foot, member, side * LANES:(side + 1) * LANES, :] = values.T * (1.0 / (SIDE * SIDE))

    def row_filter(half, part, exchanges):
        foot = 1 - half
        for slot in range(SLOTS):
            lanes = slice(slot * LANES, (slot + 1) * LANES)
            high, low = split(x_in[half, part, :, :, :, slot].reshape(ROWS, LANES))
            for base in (0, ROWS):
                x_hi[base:base + ROWS, lanes] = high
                x_lo[base:base + ROWS, lanes] = low
        for i, owner in enumerate(x_peers + [row]):
            rows = pl.ds(pl.multiple_of(owner * LANES, LANES), ROWS)
            result = dot_split((circ_hi[foot], circ_lo[foot]), (x_hi[rows, :], x_lo[rows, :]))
            for slot in range(SLOTS):
                x_res[half, part, owner, :, :, slot] = result[:, slot * LANES:(slot + 1) * LANES].reshape(
                    PARTS, PAIRS, 8, LANES
                )
            copies = exchanges[0]
            (copies[0] + [copies[1]])[i].start()
        for exchange in exchanges[1:]:
            start(exchange)

    def col_filter(half, part):
        foot = half
        forward = (matrices[0], matrices[1])
        inverse = (matrices[2], matrices[3])
        cos, sin = turns[0], turns[1]
        gain_real, gain_imag = gains[foot, 0], gains[foot, 1]

        def load_line(line):
            return jnp.concatenate(
                [yz_in[half, part, :, :, line, side].reshape(SIDE, LANES) for side in range(HALVES)], 1
            )

        def store_line(line, values):
            for side in range(HALVES):
                yz_res[half, part, :, :, line, side] = values[:, side * LANES:(side + 1) * LANES].reshape(
                    PAIRS, PARTS, STRIPS, LANES
                )

        for line in range(0, LINES, 2):
            field = jnp.concatenate([load_line(line), load_line(line + 1)], 0)
            result = dot_split(forward, split(field))
            real, imag = result[:SIDE], result[SIDE:]
            field = jnp.concatenate([real * cos + imag * sin, imag * cos - real * sin], 1)
            result = dot_split(split(field), inverse)
            real, imag = result[:, :SIDE], result[:, SIDE:]
            field = jnp.concatenate(
                [real * gain_real - imag * gain_imag, real * gain_imag + imag * gain_real], 1
            )
            result = dot_split(split(field), forward)
            real, imag = result[:, :SIDE], result[:, SIDE:]
            field = jnp.concatenate([real * cos - imag * sin, imag * cos + real * sin], 0)
            result = dot_split(inverse, split(field))
            store_line(line, result[:SIDE])
            store_line(line + 1, result[SIDE:])

    def share(owner, part):
        return pl.ds(SLOTS * (PARTS * owner + part), SLOTS)

    def yz_into(half, part):
        return yz_copies(
            half, 0, part, lambda peer: yz_pack.at[half, part, peer // PARTS, peer % PARTS],
            yz_in.at[half, part, col // PARTS, col % PARTS], yz_in.at[half, part],
        )

    def yz_return(half, part):
        return yz_copies(
            half, 1, part, lambda peer: yz_res.at[half, part, peer // PARTS, peer % PARTS],
            yz_back.at[half, part, col // PARTS, col % PARTS], yz_back.at[half, part],
        )

    parts = range(PARTS)
    others = pl.ds(0, ROW_DEVICES - 1)
    half_blocks = pl.ds(0, BLOCKS // PARTS)

    yz_first = [yz_into(0, part) for part in parts]
    x_first = [
        x_copies(
            0, 0, part, 0, lambda peer: elev.at[:, :, share(peer, part)], x_in.at[0, part, row],
            x_in.at[0, part], x_in.at[0, part, others],
        )
        for part in parts
    ]
    loads[0].wait()
    for part in parts:
        pack_natural(part)
    pl.semaphore_wait(barrier, len(YZ_STEPS) + len(X_STEPS))
    for part in parts:
        for copy in interleave(yz_first[part][0], x_first[part][0]):
            copy.start()
        yz_first[part][1].start()
        x_first[part][1].start()
    for load in loads[1:]:
        load.wait()
    for foot in range(2):
        build_circulant(foot)
        build_gains(foot)
    yz_second, x_second = [], []
    for part in parts:
        wait(x_first[part])
        x_second.append([
            x_copies(
                0, 1, part, band, lambda peer: x_res.at[0, part, peer, band],
                row_mid.at[band, :, share(row, part)], row_mid.at[band, :, half_blocks],
                x_res.at[0, part, others, band],
            )
            for band in parts
        ])
        row_filter(0, part, x_second[part])
        wait(yz_first[part])
        col_filter(0, part)
        yz_second.append(yz_return(0, part))
        start(yz_second[part])

    yz_third = [yz_into(1, part) for part in parts]
    x_third = [
        [
            x_copies(
                1, 0, part, band, lambda peer: col_mid.at[band, :, share(peer, part)],
                x_in.at[1, part, row, band], x_in.at[1, part, :, band], x_in.at[1, part, others, band],
            )
            for part in parts
        ]
        for band in parts
    ]

    def x_again(band):
        wait(yz_second[band])
        unpack_banded(band)
        for part in parts:
            start(x_third[band][part])

    def yz_again(band):
        for part in parts:
            wait(x_second[part][band])
        pack_banded(band)
        start(yz_third[band])

    x_again(0)
    yz_again(0)
    yz_again(1)
    x_again(1)
    yz_fourth = [yz_return(1, part) for part in parts]
    x_fourth = [
        x_copies(
            1, 1, part, 0, lambda peer: x_res.at[1, part, peer], out.at[0, :, :, share(row, part)],
            out.at[0, :, :, half_blocks], x_res.at[1, part, others],
        )
        for part in parts
    ]

    def columns_again(part):
        wait(yz_third[part])
        col_filter(1, part)
        start(yz_fourth[part])

    def rows_again(part):
        for band in parts:
            wait(x_third[band][part])
        row_filter(1, part, [x_fourth[part]])

    columns_again(0)
    rows_again(0)
    rows_again(1)
    columns_again(1)
    wait_sent(yz_first + x_first + yz_second + yz_third + sum(x_second + x_third, []))
    for part in parts:
        wait(yz_fourth[part])
        unpack_natural(part)
    for part in parts:
        wait(x_fourth[part])
    wait_sent(yz_fourth + x_fourth)


def finish_kernel(result, out, sems):
    pieces = [
        pltpu.make_async_copy(result.at[foot, band], out.at[foot, band], sems.at[foot, band])
        for foot in range(2)
        for band in range(PARTS)
    ]
    for piece in pieces:
        piece.start()
    for piece in pieces:
        piece.wait()


def body(elevation, row_spectra, col_spectra):
    tiles = elevation.reshape(PARTS, PAIRS, 8, BLOCKS, LANES).transpose(0, 1, 3, 2, 4)
    row_lines = row_spectra.reshape(2, 2, ROWS // LANES, LANES).transpose(0, 2, 1, 3)
    col_lines = col_spectra.reshape(2, 2, SIDE * HALVES, LANES).transpose(0, 2, 1, 3)
    inputs = [
        tiles,
        row_lines.reshape(2, 2 * ROWS // LANES, LANES),
        col_lines.reshape(2, 2 * SIDE * HALVES, LANES),
    ] + [jnp.asarray(table) for table in dft_constants()]
    field = (PARTS, PAIRS, BLOCKS, 8, LANES)
    packed = (PARTS, PAIRS, PARTS, LINES, HALVES, STRIPS, LANES)
    slots = (PARTS, ROW_DEVICES, PARTS, PAIRS, SLOTS, 8, LANES)
    hbm = pl.BlockSpec(memory_space=pltpu.HBM)
    vmem = pl.BlockSpec(memory_space=pltpu.VMEM)
    result = pl.pallas_call(
        kernel,
        out_shape=pltpu.VMEM((2,) + field, jnp.float32),
        in_specs=[hbm] * len(inputs),
        out_specs=vmem,
        scratch_shapes=[pltpu.VMEM(member.shape, member.dtype) for member in inputs] + [
            pltpu.VMEM((2, 2, SIDE, SIDE), jnp.float32),
            pltpu.VMEM((2, LANES, ROWS), jnp.bfloat16),
            pltpu.VMEM((2, LANES, ROWS), jnp.bfloat16),
            pltpu.VMEM((2,) + packed, jnp.float32),
            pltpu.VMEM((2,) + packed, jnp.float32),
            pltpu.VMEM((2,) + packed, jnp.float32),
            pltpu.VMEM((2,) + packed, jnp.float32),
            pltpu.VMEM(field, jnp.float32),
            pltpu.VMEM((2,) + slots, jnp.float32),
            pltpu.VMEM((2,) + slots, jnp.float32),
            pltpu.VMEM(field, jnp.float32),
            pltpu.VMEM((2 * ROWS, SLOTS * LANES), jnp.bfloat16),
            pltpu.VMEM((2 * ROWS, SLOTS * LANES), jnp.bfloat16),
            pltpu.SemaphoreType.DMA((2, 2, PARTS)),
            pltpu.SemaphoreType.DMA((2, 2, PARTS)),
            pltpu.SemaphoreType.DMA((2, 2, PARTS, PARTS)),
            pltpu.SemaphoreType.DMA((2, 2, PARTS, PARTS)),
            pltpu.SemaphoreType.DMA((len(inputs),)),
        ],
        compiler_params=pltpu.CompilerParams(
            collective_id=0, has_side_effects=True, vmem_limit_bytes=52 * 2**20
        ),
    )(*inputs)
    result = pl.pallas_call(
        finish_kernel,
        out_shape=jax.ShapeDtypeStruct((2,) + field, jnp.float32),
        in_specs=[vmem],
        out_specs=pl.BlockSpec(memory_space=pltpu.HBM),
        scratch_shapes=[pltpu.SemaphoreType.DMA((2, PARTS))],
        compiler_params=pltpu.CompilerParams(vmem_limit_bytes=2**20),
    )(result)
    result = result.reshape(2, TILES, BLOCKS, 8, LANES)
    return result.transpose(0, 1, 3, 2, 4).reshape((2,) + elevation.shape)


def solution(mesh):
    in_specs = (P("row", "col"), P(), P())
    out_specs = P(None, "row", "col")
    return jax.shard_map(body, mesh=mesh, in_specs=in_specs, out_specs=out_specs, check_vma=False)
```

time: 117 us -> 112 us (0.957)
  Pallas kernels: 116 us -> 111 us
    pallas_call x2, Pallas kernels: 116 us -> 111 us  [the longest x1 109 us: body(): pl.pallas_call(kernel, out_shape=pltpu.VMEM((2,) + field, jnp.float32), i...]
where the time goes in v3:
time: 112 us; the launch traced here: 111 us
  Pallas kernels  111 us (99%)
    pallas_call x1, Pallas kernels, body(): pl.pallas_call(kernel, out_shape=pltpu.VMEM((2,) + field, jnp.float32), i...  109 us

profile of v3, /device:TPU:1, one launch (start us, length us, event | category | flops | bytes accessed | tf_op | source)
XLA Modules:
  0.0 111.4 jit_solution(15035366588318450311)
XLA Ops:
  0.0 109.2 %shard_map.73.result = f32[2,2,8,32,8,128]{5,4,3,2,1,0:T(8,128)S(1)} custom-call(f32[2,8,32,8,128]{4,3,2,1,0:T(8,128)} %bitcast.18, f32[2,16,128]{2,1,0:T(8,128)} %bitcast.20, f32[2,1024,128]{2,1,0:T(8,128)} %bitcast.19, bf16[4,512,512]{2,1,0:T(8,128)(2,1)} %constant.8.clone.matrices_hbm, f32[2,256,256]{2,1,0:T(8,128)} %constant.9.clone.turns_hbm, ...), custom_call_target="tpu_custom_call" | custom-call | tf_op jit(solution)/shard_map/pallas_call | solution.py:426
  109.2 2.0 %shard_map.74 = f32[2,2,8,32,8,128]{5,4,3,2,1,0:T(8,128)} custom-call(f32[2,2,8,32,8,128]{5,4,3,2,1,0:T(8,128)S(1)} %shard_map.73.result), custom_call_target="tpu_custom_call" | custom-call | tf_op jit(solution)/shard_map/pallas_call | solution.py:455

commit v4 on v3

--- a/solution.py
+++ b/solution.py
@@ -17,8 +17,10 @@
 BLOCKS = LOCAL_COLS // LANES
 TILES = ROWS // ROW_DEVICES // 8
 PARTS = 2
+PIECES = 4
 SLOTS = BLOCKS // ROW_DEVICES // PARTS
-LINES = 8 // PARTS
+BAND = 8 // PARTS
+LINES = 8 // PIECES
 HALVES = SIDE // LANES
 STRIPS = LOCAL_COLS // SIDE
 PAIRS = TILES // PARTS
@@ -115,8 +117,8 @@
     for load in loads:
         load.start()
 
-    def yz_copies(half, stage, part, source, target, arrived):
-        sent, received = yz_send.at[half, stage, part], yz_recv.at[half, stage, part]
+    def yz_copies(half, stage, piece, source, target, arrived):
+        sent, received = yz_send.at[half, stage, piece], yz_recv.at[half, stage, piece]
         copies = [
             pltpu.make_async_remote_copy(
                 src_ref=source(peer), dst_ref=target, send_sem=sent, recv_sem=received,
@@ -124,7 +126,7 @@
             )
             for peer in yz_peers
         ]
-        shares = yz_pack.at[half, part].reshape(COL_DEVICES, LINES * HALVES, STRIPS, LANES)
+        shares = yz_pack.at[half, piece].reshape(COL_DEVICES, LINES * HALVES, STRIPS, LANES)
         leaving = shares.at[pl.ds(0, COL_DEVICES - 1)]
         return (
             copies, pltpu.make_async_copy(source(col), target, received),
@@ -156,37 +158,38 @@
         for exchange in exchanges:
             exchange[3].wait()
 
-    def natural(part):
+    def natural(piece):
         for line in range(LINES):
             for side in range(HALVES):
-                yield line, side, pl.ds(8 * side + LINES * part + line, SIDE, stride=8 * HALVES)
-
-    def banded():
+                yield line, side, pl.ds(8 * side + LINES * piece + line, SIDE, stride=8 * HALVES)
+
+    def banded(piece):
+        begin = LINES * piece % BAND
         for turn in range(PARTS):
             for line in range(LINES):
                 for side in range(HALVES):
-                    where = pl.ds(8 * side + LINES * turn + line, SIDE // PARTS, stride=8 * HALVES)
+                    where = pl.ds(8 * side + BAND * turn + begin + line, SIDE // PARTS, stride=8 * HALVES)
                     yield turn, line, side, where
 
-    def pack_natural(part):
+    def pack_natural(piece):
         rows = elev.reshape(SIDE * 8 * HALVES, LANES)
-        for line, side, where in natural(part):
-            yz_pack[0, part, :, :, line, side] = rows[where, :].reshape(PAIRS, PARTS, STRIPS, LANES)
-
-    def pack_banded(part):
-        rows = row_mid.at[part].reshape(PAIRS * BLOCKS * 8, LANES)
-        for turn, line, side, where in banded():
-            yz_pack[1, part, :, turn, line, side] = rows[where, :].reshape(PAIRS, STRIPS, LANES)
-
-    def unpack_banded(part):
-        rows = col_mid.at[part].reshape(PAIRS * BLOCKS * 8, LANES)
-        for turn, line, side, where in banded():
-            rows[where, :] = yz_back[0, part, :, turn, line, side].reshape(SIDE // PARTS, LANES)
-
-    def unpack_natural(part):
+        for line, side, where in natural(piece):
+            yz_pack[0, piece, :, :, line, side] = rows[where, :].reshape(PAIRS, PARTS, STRIPS, LANES)
+
+    def pack_banded(piece):
+        rows = row_mid.at[LINES * piece // BAND].reshape(PAIRS * BLOCKS * 8, LANES)
+        for turn, line, side, where in banded(piece):
+            yz_pack[1, piece, :, turn, line, side] = rows[where, :].reshape(PAIRS, STRIPS, LANES)
+
+    def unpack_banded(piece):
+        rows = col_mid.at[LINES * piece // BAND].reshape(PAIRS * BLOCKS * 8, LANES)
+        for turn, line, side, where in banded(piece):
+            rows[where, :] = yz_back[0, piece, :, turn, line, side].reshape(SIDE // PARTS, LANES)
+
+    def unpack_natural(piece):
         rows = out.at[1].reshape(SIDE * 8 * HALVES, LANES)
-        for line, side, where in natural(part):
-            rows[where, :] = yz_back[1, part, :, :, line, side].reshape(SIDE, LANES)
+        for line, side, where in natural(piece):
+            rows[where, :] = yz_back[1, piece, :, :, line, side].reshape(SIDE, LANES)
 
     def build_circulant(foot):
         real = row_spec[foot, pl.ds(0, 8, stride=2), :]
@@ -206,13 +209,13 @@
         rolled = pltpu.roll(jnp.broadcast_to(profile, (LANES, ROWS)), 0, 1, stride=1, stride_axis=0)
         banded_row = lax.broadcasted_iota(jnp.int32, (LANES, LANES), 0)
         natural_row = lax.broadcasted_iota(jnp.int32, (LANES, LANES), 1)
-        source = banded_row % 64 // LINES * 8 + banded_row // 64 * LINES + banded_row % LINES
+        source = banded_row % 64 // BAND * 8 + banded_row // 64 * BAND + banded_row % BAND
         for target, values in zip((circ_hi, circ_lo), split(rolled)):
             if foot == 1:
                 order = jnp.where(source == natural_row, 1.0, 0.0).astype(jnp.bfloat16)
                 target[foot] = dot(order, values).astype(jnp.bfloat16)
             else:
-                source_column = natural_row % 64 // LINES * 8 + natural_row // 64 * LINES + natural_row % LINES
+                source_column = natural_row % 64 // BAND * 8 + natural_row // 64 * BAND + natural_row % BAND
                 order = jnp.where(source_column == banded_row, 1.0, 0.0).astype(jnp.bfloat16)
                 for block in range(ROW_DEVICES):
                     lanes = slice(block * LANES, (block + 1) * LANES)
@@ -244,7 +247,7 @@
         for exchange in exchanges[1:]:
             start(exchange)
 
-    def col_filter(half, part):
+    def col_filter(half, piece):
         foot = half
         forward = (matrices[0], matrices[1])
         inverse = (matrices[2], matrices[3])
@@ -253,12 +256,12 @@
 
         def load_line(line):
             return jnp.concatenate(
-                [yz_in[half, part, :, :, line, side].reshape(SIDE, LANES) for side in range(HALVES)], 1
+                [yz_in[half, piece, :, :, line, side].reshape(SIDE, LANES) for side in range(HALVES)], 1
             )
 
         def store_line(line, values):
             for side in range(HALVES):
-                yz_res[half, part, :, :, line, side] = values[:, side * LANES:(side + 1) * LANES].reshape(
+                yz_res[half, piece, :, :, line, side] = values[:, side * LANES:(side + 1) * LANES].reshape(
                     PAIRS, PARTS, STRIPS, LANES
                 )
 
@@ -282,23 +285,24 @@
     def share(owner, part):
         return pl.ds(SLOTS * (PARTS * owner + part), SLOTS)
 
-    def yz_into(half, part):
+    def yz_into(half, piece):
         return yz_copies(
-            half, 0, part, lambda peer: yz_pack.at[half, part, peer // PARTS, peer % PARTS],
-            yz_in.at[half, part, col // PARTS, col % PARTS], yz_in.at[half, part],
-        )
-
-    def yz_return(half, part):
+            half, 0, piece, lambda peer: yz_pack.at[half, piece, peer // PARTS, peer % PARTS],
+            yz_in.at[half, piece, col // PARTS, col % PARTS], yz_in.at[half, piece],
+        )
+
+    def yz_return(half, piece):
         return yz_copies(
-            half, 1, part, lambda peer: yz_res.at[half, part, peer // PARTS, peer % PARTS],
-            yz_back.at[half, part, col // PARTS, col % PARTS], yz_back.at[half, part],
+            half, 1, piece, lambda peer: yz_res.at[half, piece, peer // PARTS, peer % PARTS],
+            yz_back.at[half, piece, col // PARTS, col % PARTS], yz_back.at[half, piece],
         )
 
     parts = range(PARTS)
+    pieces = range(PIECES)
     others = pl.ds(0, ROW_DEVICES - 1)
     half_blocks = pl.ds(0, BLOCKS // PARTS)
 
-    yz_first = [yz_into(0, part) for part in parts]
+    yz_first = [yz_into(0, piece) for piece in pieces]
     x_first = [
         x_copies(
             0, 0, part, 0, lambda peer: elev.at[:, :, share(peer, part)], x_in.at[0, part, row],
@@ -307,37 +311,53 @@
         for part in parts
     ]
     loads[0].wait()
-    for part in parts:
-        pack_natural(part)
+    for piece in pieces[:2]:
+        pack_natural(piece)
     pl.semaphore_wait(barrier, len(YZ_STEPS) + len(X_STEPS))
     for part in parts:
-        for copy in interleave(yz_first[part][0], x_first[part][0]):
+        members = yz_first[2 * part:2 * part + 2]
+        for copy in interleave(members[0][0] + members[1][0], x_first[part][0]):
             copy.start()
-        yz_first[part][1].start()
-        x_first[part][1].start()
+        for exchange in members + [x_first[part]]:
+            exchange[1].start()
+        if part == 0:
+            for piece in pieces[2:]:
+                pack_natural(piece)
     for load in loads[1:]:
         load.wait()
     for foot in range(2):
         build_circulant(foot)
         build_gains(foot)
-    yz_second, x_second = [], []
-    for part in parts:
-        wait(x_first[part])
-        x_second.append([
+    yz_second = [yz_return(0, piece) for piece in pieces]
+    x_second = [
+        [
             x_copies(
                 0, 1, part, band, lambda peer: x_res.at[0, part, peer, band],
                 row_mid.at[band, :, share(row, part)], row_mid.at[band, :, half_blocks],
                 x_res.at[0, part, others, band],
             )
             for band in parts
-        ])
+        ]
+        for part in parts
+    ]
+
+    def rows_once(part):
+        wait(x_first[part])
         row_filter(0, part, x_second[part])
-        wait(yz_first[part])
-        col_filter(0, part)
-        yz_second.append(yz_return(0, part))
-        start(yz_second[part])
-
-    yz_third = [yz_into(1, part) for part in parts]
+
+    def columns_once(piece):
+        wait(yz_first[piece])
+        col_filter(0, piece)
+        start(yz_second[piece])
+
+    columns_once(0)
+    rows_once(0)
+    columns_once(1)
+    columns_once(2)
+    rows_once(1)
+    columns_once(3)
+
+    yz_third = [yz_into(1, piece) for piece in pieces]
     x_third = [
         [
             x_copies(
@@ -350,22 +370,24 @@
     ]
 
     def x_again(band):
-        wait(yz_second[band])
-        unpack_banded(band)
+        for piece in pieces[2 * band:2 * band + 2]:
+            wait(yz_second[piece])
+            unpack_banded(piece)
         for part in parts:
             start(x_third[band][part])
 
     def yz_again(band):
         for part in parts:
             wait(x_second[part][band])
-        pack_banded(band)
-        start(yz_third[band])
+        for piece in pieces[2 * band:2 * band + 2]:
+            pack_banded(piece)
+            start(yz_third[piece])
 
     x_again(0)
     yz_again(0)
     yz_again(1)
     x_again(1)
-    yz_fourth = [yz_return(1, part) for part in parts]
+    yz_fourth = [yz_return(1, piece) for piece in pieces]
     x_fourth = [
         x_copies(
             1, 1, part, 0, lambda peer: x_res.at[1, part, peer], out.at[0, :, :, share(row, part)],
@@ -374,10 +396,10 @@
         for part in parts
     ]
 
-    def columns_again(part):
-        wait(yz_third[part])
-        col_filter(1, part)
-        start(yz_fourth[part])
+    def columns_again(piece):
+        wait(yz_third[piece])
+        col_filter(1, piece)
+        start(yz_fourth[piece])
 
     def rows_again(part):
         for band in parts:
@@ -385,13 +407,15 @@
         row_filter(1, part, [x_fourth[part]])
 
     columns_again(0)
+    columns_again(1)
     rows_again(0)
+    columns_again(2)
     rows_again(1)
-    columns_again(1)
+    columns_again(3)
     wait_sent(yz_first + x_first + yz_second + yz_third + sum(x_second + x_third, []))
-    for part in parts:
-        wait(yz_fourth[part])
-        unpack_natural(part)
+    for piece in pieces:
+        wait(yz_fourth[piece])
+        unpack_natural(piece)
     for part in parts:
         wait(x_fourth[part])
     wait_sent(yz_fourth + x_fourth)
@@ -419,7 +443,7 @@
         col_lines.reshape(2, 2 * SIDE * HALVES, LANES),
     ] + [jnp.asarray(table) for table in dft_constants()]
     field = (PARTS, PAIRS, BLOCKS, 8, LANES)
-    packed = (PARTS, PAIRS, PARTS, LINES, HALVES, STRIPS, LANES)
+    packed = (PIECES, PAIRS, PARTS, LINES, HALVES, STRIPS, LANES)
     slots = (PARTS, ROW_DEVICES, PARTS, PAIRS, SLOTS, 8, LANES)
     hbm = pl.BlockSpec(memory_space=pltpu.HBM)
     vmem = pl.BlockSpec(memory_space=pltpu.VMEM)
@@ -442,8 +466,8 @@
             pltpu.VMEM(field, jnp.float32),
             pltpu.VMEM((2 * ROWS, SLOTS * LANES), jnp.bfloat16),
             pltpu.VMEM((2 * ROWS, SLOTS * LANES), jnp.bfloat16),
-            pltpu.SemaphoreType.DMA((2, 2, PARTS)),
-            pltpu.SemaphoreType.DMA((2, 2, PARTS)),
+            pltpu.SemaphoreType.DMA((2, 2, PIECES)),
+            pltpu.SemaphoreType.DMA((2, 2, PIECES)),
             pltpu.SemaphoreType.DMA((2, 2, PARTS, PARTS)),
             pltpu.SemaphoreType.DMA((2, 2, PARTS, PARTS)),
             pltpu.SemaphoreType.DMA((len(inputs),)),

time: 112 us -> 104 us (0.929)
  Pallas kernels: 111 us -> 104 us
    pallas_call x1, Pallas kernels: 109 us -> 102 us  [body(): pl.pallas_call(kernel, out_shape=pltpu.VMEM((2,) + field, jnp.float32), i...]
where the time goes in v4:
time: 104 us
  Pallas kernels  104 us (100%)
    pallas_call x1, Pallas kernels, body(): pl.pallas_call(kernel, out_shape=pltpu.VMEM((2,) + field, jnp.float32), i...  102 us

profile of v4, /device:TPU:1, one launch (start us, length us, event | category | flops | bytes accessed | tf_op | source)
XLA Modules:
  0.0 103.8 jit_solution(7817493142382167525)
XLA Ops:
  0.0 101.6 %shard_map.73.result = f32[2,2,8,32,8,128]{5,4,3,2,1,0:T(8,128)S(1)} custom-call(f32[2,8,32,8,128]{4,3,2,1,0:T(8,128)} %bitcast.18, f32[2,16,128]{2,1,0:T(8,128)} %bitcast.20, f32[2,1024,128]{2,1,0:T(8,128)} %bitcast.19, bf16[4,512,512]{2,1,0:T(8,128)(2,1)} %constant.8.clone.matrices_hbm, f32[2,256,256]{2,1,0:T(8,128)} %constant.9.clone.turns_hbm, ...), custom_call_target="tpu_custom_call" | custom-call | tf_op jit(solution)/shard_map/pallas_call | solution.py:450
  101.6 2.0 %shard_map.74 = f32[2,2,8,32,8,128]{5,4,3,2,1,0:T(8,128)} custom-call(f32[2,2,8,32,8,128]{5,4,3,2,1,0:T(8,128)S(1)} %shard_map.73.result), custom_call_target="tpu_custom_call" | custom-call | tf_op jit(solution)/shard_map/pallas_call | solution.py:479

commit v5 on v4

--- a/solution.py
+++ b/solution.py
@@ -24,6 +24,10 @@
 HALVES = SIDE // LANES
 STRIPS = LOCAL_COLS // SIDE
 PAIRS = TILES // PARTS
+X_CUTS = 1
+GROUPS = [[(0,), (1,), (2,), (3,)]] * 4
+FIRST_ORDER = ["c0", "r0", "c1", "c2", "r1", "c3"]
+SECOND_ORDER = ["c0", "c1", "r0", "c2", "r1", "c3"]
 YZ_STEPS = [
     (1, 1), (3, 3), (2, 2), (1, 3), (3, 1), (2, 1), (1, 2), (2, 3),
     (3, 2), (2, 0), (0, 2), (1, 0), (0, 1), (3, 0), (0, 3),
@@ -117,30 +121,39 @@
     for load in loads:
         load.start()
 
-    def yz_copies(half, stage, piece, source, target, arrived):
-        sent, received = yz_send.at[half, stage, piece], yz_recv.at[half, stage, piece]
+    def yz_copies(half, stage, group, source, target):
+        sent, received = yz_send.at[half, stage, group[0]], yz_recv.at[half, stage, group[0]]
+        count = len(group)
+        pieces = pl.ds(group[0], count)
+
+        def piece_of(field, peer):
+            return field.at[half, pieces, peer // PARTS, peer % PARTS]
+
         copies = [
             pltpu.make_async_remote_copy(
-                src_ref=source(peer), dst_ref=target, send_sem=sent, recv_sem=received,
-                device_id=(row, peer), device_id_type=MESH,
+                src_ref=piece_of(source, peer), dst_ref=piece_of(target, col), send_sem=sent,
+                recv_sem=received, device_id=(row, peer), device_id_type=MESH,
             )
             for peer in yz_peers
         ]
-        shares = yz_pack.at[half, piece].reshape(COL_DEVICES, LINES * HALVES, STRIPS, LANES)
-        leaving = shares.at[pl.ds(0, COL_DEVICES - 1)]
+        arrived = target.at[half, pieces]
+        shares = source.at[half, pieces].reshape(count * COL_DEVICES, LINES * HALVES, STRIPS, LANES)
+        leaving = shares.at[pl.ds(0, count * (COL_DEVICES - 1))]
         return (
-            copies, pltpu.make_async_copy(source(col), target, received),
+            copies, pltpu.make_async_copy(piece_of(source, col), piece_of(target, col), received),
             pltpu.make_async_copy(arrived, arrived, received), pltpu.make_async_copy(leaving, leaving, sent),
         )
 
     def x_copies(half, stage, part, band, source, target, arrived, leaving):
         sent, received = x_send.at[half, stage, part, band], x_recv.at[half, stage, part, band]
+        cuts = [pl.ds(cut * PAIRS // X_CUTS, PAIRS // X_CUTS) for cut in range(X_CUTS)]
         copies = [
             pltpu.make_async_remote_copy(
-                src_ref=source(peer), dst_ref=target, send_sem=sent, recv_sem=received,
+                src_ref=source(peer).at[cut], dst_ref=target.at[cut], send_sem=sent, recv_sem=received,
                 device_id=(peer, col), device_id_type=MESH,
             )
             for peer in x_peers
+            for cut in cuts
         ]
         return (
             copies, pltpu.make_async_copy(source(row), target, received),
@@ -242,8 +255,9 @@
                 x_res[half, part, owner, :, :, slot] = result[:, slot * LANES:(slot + 1) * LANES].reshape(
                     PARTS, PAIRS, 8, LANES
                 )
-            copies = exchanges[0]
-            (copies[0] + [copies[1]])[i].start()
+            copies = exchanges[0][0][i * X_CUTS:(i + 1) * X_CUTS]
+            for copy in copies if i < len(x_peers) else [exchanges[0][1]]:
+                copy.start()
         for exchange in exchanges[1:]:
             start(exchange)
 
@@ -285,29 +299,34 @@
     def share(owner, part):
         return pl.ds(SLOTS * (PARTS * owner + part), SLOTS)
 
-    def yz_into(half, piece):
-        return yz_copies(
-            half, 0, piece, lambda peer: yz_pack.at[half, piece, peer // PARTS, peer % PARTS],
-            yz_in.at[half, piece, col // PARTS, col % PARTS], yz_in.at[half, piece],
-        )
-
-    def yz_return(half, piece):
-        return yz_copies(
-            half, 1, piece, lambda peer: yz_res.at[half, piece, peer // PARTS, peer % PARTS],
-            yz_back.at[half, piece, col // PARTS, col % PARTS], yz_back.at[half, piece],
-        )
+    def yz_exchange(half, stage):
+        source, target = ((yz_pack, yz_in), (yz_res, yz_back))[stage]
+        return {group: yz_copies(half, stage, group, source, target) for group in GROUPS[2 * half + stage]}
+
+    def wait_piece(exchange, piece):
+        for group in exchange:
+            if group[0] == piece:
+                wait(exchange[group])
+
+    def start_piece(exchange, piece):
+        for group in exchange:
+            if group[-1] == piece:
+                start(exchange[group])
 
     parts = range(PARTS)
     pieces = range(PIECES)
     others = pl.ds(0, ROW_DEVICES - 1)
     half_blocks = pl.ds(0, BLOCKS // PARTS)
 
-    yz_first = [yz_into(0, piece) for piece in pieces]
+    yz_first = yz_exchange(0, 0)
     x_first = [
-        x_copies(
-            0, 0, part, 0, lambda peer: elev.at[:, :, share(peer, part)], x_in.at[0, part, row],
-            x_in.at[0, part], x_in.at[0, part, others],
-        )
+        [
+            x_copies(
+                0, 0, part, band, lambda peer: elev.at[band, :, share(peer, part)],
+                x_in.at[0, part, row, band], x_in.at[0, part, :, band], x_in.at[0, part, others, band],
+            )
+            for band in parts
+        ]
         for part in parts
     ]
     loads[0].wait()
@@ -315,10 +334,12 @@
         pack_natural(piece)
     pl.semaphore_wait(barrier, len(YZ_STEPS) + len(X_STEPS))
     for part in parts:
-        members = yz_first[2 * part:2 * part + 2]
-        for copy in interleave(members[0][0] + members[1][0], x_first[part][0]):
+        members = [yz_first[group] for group in yz_first if group[0] // 2 == part]
+        for copy in interleave(
+            sum((member[0] for member in members), []), x_first[part][0][0] + x_first[part][1][0]
+        ):
             copy.start()
-        for exchange in members + [x_first[part]]:
+        for exchange in members + x_first[part]:
             exchange[1].start()
         if part == 0:
             for piece in pieces[2:]:
@@ -328,7 +349,7 @@
     for foot in range(2):
         build_circulant(foot)
         build_gains(foot)
-    yz_second = [yz_return(0, piece) for piece in pieces]
+    yz_second = yz_exchange(0, 1)
     x_second = [
         [
             x_copies(
@@ -342,22 +363,19 @@
     ]
 
     def rows_once(part):
-        wait(x_first[part])
+        for band in parts:
+            wait(x_first[part][band])
         row_filter(0, part, x_second[part])
 
     def columns_once(piece):
-        wait(yz_first[piece])
+        wait_piece(yz_first, piece)
         col_filter(0, piece)
-        start(yz_second[piece])
-
-    columns_once(0)
-    rows_once(0)
-    columns_once(1)
-    columns_once(2)
-    rows_once(1)
-    columns_once(3)
-
-    yz_third = [yz_into(1, piece) for piece in pieces]
+        start_piece(yz_second, piece)
+
+    for step in FIRST_ORDER:
+        (columns_once if step[0] == "c" else rows_once)(int(step[1]))
+
+    yz_third = yz_exchange(1, 0)
     x_third = [
         [
             x_copies(
@@ -371,7 +389,7 @@
 
     def x_again(band):
         for piece in pieces[2 * band:2 * band + 2]:
-            wait(yz_second[piece])
+            wait_piece(yz_second, piece)
             unpack_banded(piece)
         for part in parts:
             start(x_third[band][part])
@@ -381,44 +399,47 @@
             wait(x_second[part][band])
         for piece in pieces[2 * band:2 * band + 2]:
             pack_banded(piece)
-            start(yz_third[piece])
+            start_piece(yz_third, piece)
 
     x_again(0)
     yz_again(0)
     yz_again(1)
     x_again(1)
-    yz_fourth = [yz_return(1, piece) for piece in pieces]
+    yz_fourth = yz_exchange(1, 1)
     x_fourth = [
-        x_copies(
-            1, 1, part, 0, lambda peer: x_res.at[1, part, peer], out.at[0, :, :, share(row, part)],
-            out.at[0, :, :, half_blocks], x_res.at[1, part, others],
-        )
+        [
+            x_copies(
+                1, 1, part, band, lambda peer: x_res.at[1, part, peer, band],
+                out.at[0, band, :, share(row, part)], out.at[0, band, :, half_blocks],
+                x_res.at[1, part, others, band],
+            )
+            for band in parts
+        ]
         for part in parts
     ]
 
     def columns_again(piece):
-        wait(yz_third[piece])
+        wait_piece(yz_third, piece)
         col_filter(1, piece)
-        start(yz_fourth[piece])
+        start_piece(yz_fourth, piece)
 
     def rows_again(part):
         for band in parts:
             wait(x_third[band][part])
-        row_filter(1, part, [x_fourth[part]])
-
-    columns_again(0)
-    columns_again(1)
-    rows_again(0)
-    columns_again(2)
-    rows_again(1)
-    columns_again(3)
-    wait_sent(yz_first + x_first + yz_second + yz_third + sum(x_second + x_third, []))
+        row_filter(1, part, x_fourth[part])
+
+    for step in SECOND_ORDER:
+        (columns_again if step[0] == "c" else rows_again)(int(step[1]))
+    for exchange in (yz_first, yz_second, yz_third):
+        wait_sent(exchange.values())
+    wait_sent(sum(x_first + x_second + x_third, []))
     for piece in pieces:
-        wait(yz_fourth[piece])
+        wait_piece(yz_fourth, piece)
         unpack_natural(piece)
-    for part in parts:
-        wait(x_fourth[part])
-    wait_sent(yz_fourth + x_fourth)
+    for exchange in sum(x_fourth, []):
+        wait(exchange)
+    wait_sent(yz_fourth.values())
+    wait_sent(sum(x_fourth, []))
 
 
 def finish_kernel(result, out, sems):

time: 104 us -> 104 us (level)
  no operation moved by 1% of the time
where the time goes in v5:
time: 104 us
  Pallas kernels  104 us (100%)
    pallas_call x1, Pallas kernels, body(): pl.pallas_call(kernel, out_shape=pltpu.VMEM((2,) + field, jnp.float32), i...  101 us

profile of v5, /device:TPU:1, one launch (start us, length us, event | category | flops | bytes accessed | tf_op | source)
XLA Modules:
  0.0 103.7 jit_solution(18246378464643513885)
XLA Ops:
  0.0 101.5 %shard_map.73.result = f32[2,2,8,32,8,128]{5,4,3,2,1,0:T(8,128)S(1)} custom-call(f32[2,8,32,8,128]{4,3,2,1,0:T(8,128)} %bitcast.18, f32[2,16,128]{2,1,0:T(8,128)} %bitcast.20, f32[2,1024,128]{2,1,0:T(8,128)} %bitcast.19, bf16[4,512,512]{2,1,0:T(8,128)(2,1)} %constant.8.clone.matrices_hbm, f32[2,256,256]{2,1,0:T(8,128)} %constant.9.clone.turns_hbm, ...), custom_call_target="tpu_custom_call" | custom-call | tf_op jit(solution)/shard_map/pallas_call | solution.py:471
  101.5 2.0 %shard_map.74 = f32[2,2,8,32,8,128]{5,4,3,2,1,0:T(8,128)} custom-call(f32[2,2,8,32,8,128]{5,4,3,2,1,0:T(8,128)S(1)} %shard_map.73.result), custom_call_target="tpu_custom_call" | custom-call | tf_op jit(solution)/shard_map/pallas_call | solution.py:500

commit v6 on v5

--- a/solution.py
+++ b/solution.py
@@ -25,7 +25,7 @@
 STRIPS = LOCAL_COLS // SIDE
 PAIRS = TILES // PARTS
 X_CUTS = 1
-GROUPS = [[(0,), (1,), (2,), (3,)]] * 4
+GROUPS = [[(0,), (1,), (2,), (3,)]] * 3 + [[(0, 1), (2,), (3,)]]
 FIRST_ORDER = ["c0", "r0", "c1", "c2", "r1", "c3"]
 SECOND_ORDER = ["c0", "c1", "r0", "c2", "r1", "c3"]
 YZ_STEPS = [
@@ -444,9 +444,8 @@
 
 def finish_kernel(result, out, sems):
     pieces = [
-        pltpu.make_async_copy(result.at[foot, band], out.at[foot, band], sems.at[foot, band])
+        pltpu.make_async_copy(result.at[foot], out.at[foot], sems.at[foot])
         for foot in range(2)
-        for band in range(PARTS)
     ]
     for piece in pieces:
         piece.start()
@@ -502,7 +501,7 @@
         out_shape=jax.ShapeDtypeStruct((2,) + field, jnp.float32),
         in_specs=[vmem],
         out_specs=pl.BlockSpec(memory_space=pltpu.HBM),
-        scratch_shapes=[pltpu.SemaphoreType.DMA((2, PARTS))],
+        scratch_shapes=[pltpu.SemaphoreType.DMA((2,))],
         compiler_params=pltpu.CompilerParams(vmem_limit_bytes=2**20),
     )(result)
     result = result.reshape(2, TILES, BLOCKS, 8, LANES)

time: 104 us -> 104 us (level)
  no operation moved by 1% of the time
where the time goes in v6:
time: 104 us
  Pallas kernels  103 us (99%)
    pallas_call x1, Pallas kernels, body(): pl.pallas_call(kernel, out_shape=pltpu.VMEM((2,) + field, jnp.float32), i...  101 us

profile of v6, /device:TPU:1, one launch (start us, length us, event | category | flops | bytes accessed | tf_op | source)
XLA Modules:
  0.0 103.7 jit_solution(6939491807393821673)
XLA Ops:
  0.0 101.5 %shard_map.73.result = f32[2,2,8,32,8,128]{5,4,3,2,1,0:T(8,128)S(1)} custom-call(f32[2,8,32,8,128]{4,3,2,1,0:T(8,128)} %bitcast.18, f32[2,16,128]{2,1,0:T(8,128)} %bitcast.20, f32[2,1024,128]{2,1,0:T(8,128)} %bitcast.19, bf16[4,512,512]{2,1,0:T(8,128)(2,1)} %constant.8.clone.matrices_hbm, f32[2,256,256]{2,1,0:T(8,128)} %constant.9.clone.turns_hbm, ...), custom_call_target="tpu_custom_call" | custom-call | tf_op jit(solution)/shard_map/pallas_call | solution.py:470
  101.5 2.0 %shard_map.74 = f32[2,2,8,32,8,128]{5,4,3,2,1,0:T(8,128)} custom-call(f32[2,2,8,32,8,128]{5,4,3,2,1,0:T(8,128)S(1)} %shard_map.73.result), custom_call_target="tpu_custom_call" | custom-call | tf_op jit(solution)/shard_map/pallas_call | solution.py:499
